TPU v7x, 256 devices: a whole 4x4x8 slice. The times are simulated.
256 devices in a mesh: snapshot: 4 (over z_lo), face: 32 (over y, x, core), row: 2 (over z_hi).
Axes of the slice: x: 4, y: 4, z: 8 (z_hi: 2, z_lo: 4; z = z_hi * 4 + z_lo), core: 2. Of those that a mesh axis runs over, the one named last changes fastest.
Arguments:
- surface_field: bfloat16 [32, 48, 48, 2048], P('face', 'row', None, 'snapshot'), may hold values from -12 to 12, as said below
- ocean_mask: int32 [32, 48, 48], P('face', 'row'), may hold values from 0 to 1, as said below
- cell_area: float32 [32, 48, 48], P('face', 'row'), may hold values from 0.25 to 4
- tile_links: int32 [32, 2], replicated, may hold values from 0 to 31
- edge_turns: int32 [32, 2], replicated, may hold values from 0 to 3
Outputs:
- anomaly: bfloat16 [32, 48, 48, 2048], P('face', 'row', None, 'snapshot')
- gram_matrix: float32 [2048, 2048], P(('snapshot', 'face', 'row'))
Inputs may be any that keep to these rules, and one draw needn't show every extreme that they name: `surface_field`: temporally correlated over a few snapshots, independent from cell to cell. `ocean_mask`: within the first 24 rows of all tiles together exactly half the cells are ocean, and likewise within the last 24 rows; land fractions differ strongly from tile to tile, and some tile is ocean in full.
All inputs are finite; a program needn't handle non-finite values.
Results may differ from a plain program's by a relative error of at most 0.001.
Values may be sent and summed in bfloat16 or wider, within the bound.
A program may use at most 64 MiB of HBM per device.

v0:
```python
import jax
import jax.numpy as jnp
from jax import lax
from jax.sharding import PartitionSpec as P

SNAPS = 2048


def per_device(surface_field, ocean_mask, cell_area, tile_links, edge_turns):
    tile_rows = surface_field.shape[1]
    tile_width = surface_field.shape[2]
    snap_block = surface_field.shape[3]
    tile_values = surface_field[0]
    west_part = tile_values[:, 0, :]
    first_row = tile_values[0]
    west_all, rows_all = (
        lax.all_gather(west_part, ("face", "row"), axis=0, tiled=True),
        lax.all_gather(first_row, ("face", "row"), axis=0, tiled=True),
    )
    tile_index = lax.axis_index("face")
    row_index = lax.axis_index("row")

    def neighbour_line(side_index):
        neighbour = tile_links[tile_index, side_index]
        turn_code = edge_turns[tile_index, side_index]
        west_line = lax.dynamic_slice_in_dim(west_all, neighbour * tile_width, tile_width, 0)
        south_line = lax.dynamic_slice_in_dim(rows_all, 2 * neighbour * tile_width, tile_width, 0)
        chosen_line = jnp.where(turn_code < 2, west_line, south_line)
        return jnp.where(turn_code % 2 == 1, chosen_line[::-1], chosen_line)

    east_line = lax.dynamic_slice_in_dim(neighbour_line(0), row_index * tile_rows, tile_rows, 0)
    inner_row = lax.dynamic_slice_in_dim(rows_all, (2 * tile_index + 1) * tile_width, tile_width, 0)
    above_row = jnp.where(row_index == 0, inner_row, neighbour_line(1))
    cell_values = tile_values.astype(jnp.float32)
    grad_cols = (
        jnp.concatenate([cell_values[:, 1:], east_line[:, None, :].astype(jnp.float32)], axis=1)
        - cell_values
    )
    grad_rows = (
        jnp.concatenate([cell_values[1:], above_row[None].astype(jnp.float32)], axis=0)
        - cell_values
    )
    area_cell = cell_area[0]
    slope_norm = jnp.sqrt(
        1.0 + (grad_cols * grad_cols + grad_rows * grad_rows) / area_cell[:, :, None]
    )
    column_sum = lax.psum(jnp.sum(slope_norm, axis=-1), "snapshot")
    column_mean = column_sum / SNAPS
    weighting = jnp.sqrt(area_cell) * ocean_mask[0].astype(jnp.float32)
    anomaly = (weighting[:, :, None] * (slope_norm - column_mean[:, :, None])).astype(jnp.bfloat16)
    ocean_points = anomaly.reshape(tile_rows * tile_width, snap_block)
    face_count = lax.axis_size("face")
    gathered = lax.all_gather(ocean_points, "snapshot", axis=1, tiled=True)
    gram_scale = 1.0 / (face_count * tile_width * tile_width)
    share_rows = snap_block // lax.axis_size(("face", "row"))
    product = lax.dot_general(
        ocean_points, gathered, (((0,), (0,)), ((), ())), preferred_element_type=jnp.float32
    )
    full_gram = lax.psum(product * gram_scale, ("face", "row"))
    gram_block = lax.dynamic_slice_in_dim(
        full_gram, lax.axis_index(("face", "row")) * share_rows, share_rows, 0
    )
    return (anomaly[None], gram_block)


def solution(mesh):
    placed = (
        P("face", "row", None, "snapshot"),
        P("face", "row", None),
        P("face", "row", None),
        P(),
        P(),
    )
    return jax.shard_map(
        per_device,
        mesh=mesh,
        in_specs=placed,
        out_specs=(P("face", "row", None, "snapshot"), P(("snapshot", "face", "row"), None)),
        check_vma=False,
    )
```

profile of v0, /device:TPU:8, one launch (start us, length us, event | category | flops | bytes accessed | tf_op | source)
XLA Modules:
  0.0 1128.3 jit_solution(1347630776468122697)
XLA Ops:
  7.2 3.6 copy_convert_fusion
  11.5 0.6 slice.15
  12.3 1.4 constant_dynamic-slice_fusion.1
  21.1 0.7 squeeze.29
  21.7 0.7 copy.29
  22.4 4.5 copy.33
  27.5 1.4 convert_element_type.54
  28.9 1.3 sqrt_multiply_fusion
  30.2 2.7 fusion.19
  32.9 2.9 fusion.18
  35.8 58.4 %all-gather.8.cloned.1.call-done = bf16[1536,1,512]{2,0,1:T(8,128)(2,1)} async-done(((bf16[24,1,512]{2,0,1:T(8,128)(2,1)}), bf16[1536,1,512]{2,0,1:T(8,128)(2,1)}) %all-gather.8.cloned.1.call-update) | async-done | bytes 1572880 | tf_op jit(solution)/shard_map/all_gather | solution.py:17
  94.2 85.7 %all-gather.10.cloned.1.call-done = bf16[1,1,3072,512]{3,2,1,0:T(8,128)(2,1)} async-done(((bf16[1,1,48,512]{3,2,1,0:T(8,128)(2,1)}), bf16[1,1,3072,512]{3,2,1,0:T(8,128)(2,1)}) %all-gather.10.cloned.1.call-update) | async-done | bytes 3145744 | tf_op jit(solution)/shard_map/all_gather | solution.py:18
  179.9 0.9 bitcast_select_fusion.2
  181.1 0.8 fusion.16
  182.0 0.6 convert_bitcast_fusion
  182.7 5.8 sqrt_reduce_fusion
  188.4 17.6 %psum.14 = f32[24,48]{0,1:T(8,128)} all-reduce(f32[24,48]{0,1:T(8,128)} %get-tuple-element.8), channel_id=1, replica_groups=mesh['snapshot'=4,'face'=32,'row'=2] {'snapshot'}, use_global_device_ids=true, to_apply=%region_1.2 | all-reduce | flops 1152 | bytes 9216 | tf_op jit(solution)/shard_map/psum | solution.py:47
  206.0 1.3 broadcast_multiply_fusion
  207.4 2.8 copy.34
  210.2 2.8 copy.32
  212.9 1.4 copy.35
  214.3 1.4 sub.42
  215.7 4.1 fusion.15
  220.1 88.9 %all-gather.6.cloned.1.call-done = bf16[1152,2048]{1,0:T(8,128)(2,1)} async-done(((bf16[1152,512]{1,0:T(8,128)(2,1)}), bf16[1152,2048]{1,0:T(8,128)(2,1)}) %all-gather.6.cloned.1.call-update) | async-done | bytes 4718608 | tf_op jit(solution)/shard_map/all_gather | solution.py:53
  309.0 7.6 convolution_multiply_fusion
  316.7 1.5 bitcast_multiply_fusion
  318.1 1.4 copy.26
  319.5 1.0 concatenate.28
  320.5 4.0 multiply_convert_fusion
  324.6 1.4 copy.36
  325.9 794.4 %all-reduce.2.cloned.1.call-done = f32[512,2048]{1,0:T(8,128)} async-done(((f32[512,2048]{1,0:T(8,128)}), f32[512,2048]{1,0:T(8,128)}) %all-reduce.2.cloned.1.call-update) | async-done | bytes 4194320 | tf_op jit(solution)/shard_map/psum | solution.py:59
  1120.3 1.5 constant_dynamic-slice_fusion
  (29 shorter events, 2.1 us)
Async XLA Ops:
  7.2 4.4 copy-start
  7.2 5.1 copy-start.7
  7.2 13.9 %copy-start.5 = (f32[1,24,48]{2,1,0:T(8,128)S(1)}, f32[1,24,48]{2,1,0:T(8,128)}, u32[]{:S(2)}) copy-start(f32[1,24,48]{2,1,0:T(8,128)} %param.7) | copy-start | bytes 13828
  7.2 87.0 %all-gather.8.cloned.1.call-start = ((), (), s32[]{:S(2)}) async-start(), calls=%async_computation.2 | async-start | bytes 1597440 | tf_op jit(solution)/shard_map/all_gather | solution.py:17
  11.5 168.4 %all-gather.10.cloned.1.call-start = ((), (), s32[]{:S(2)}) async-start(), calls=%async_computation.3 | async-start | bytes 3194880 | tf_op jit(solution)/shard_map/all_gather | solution.py:18
  12.2 296.8 %all-gather.6.cloned.1.call-start = ((), (), s32[]{:S(2)}) async-start(), calls=%async_computation | async-start | bytes 5898240 | tf_op jit(solution)/shard_map/all_gather | solution.py:53
  22.4 4.5 copy-start.6
  181.9 0.8 copy-start.4
  207.3 2.8 copy-start.3
  210.2 5.6 copy-start.1
  219.9 900.5 %all-reduce.2.cloned.1.call-start = ((), (), s32[]{:S(2)}) async-start(), calls=%async_computation.1 | async-start | bytes 8388608 | tf_op jit(solution)/shard_map/psum | solution.py:59
  316.6 3.9 copy-start.2
Sparse Core Ops, SparseCore 0:
  12.4 81.7 all-gather.7
  98.5 81.3 all-gather.9
  220.0 88.9 all-gather.5
  316.8 803.4 all-reduce.1
where the time goes:
time: 1150 us; the launch traced here: 1130 us
  waiting for transfers between devices  1030 us (90%)
  local copies, waits for them, and re-layouts  29.4 us (3%)
  other arithmetic  24.6 us (2%)
  between operations  21.2 us (2%)
  blocking collectives  17.6 us (2%)
    psum x1, waiting for transfers between devices, per_device(): full_gram = lax.psum(product * gram_scale, ('face', 'row'))  794 us
    all_gather x1, waiting for transfers between devices, per_device(): gathered = lax.all_gather(ocean_points, 'snapshot', axis=1, tiled=True)  88.9 us
    all_gather x1, waiting for transfers between devices, per_device(): lax.all_gather(first_row, ('face', 'row'), axis=0, tiled=True)  85.7 us
    all_gather x1, waiting for transfers between devices, per_device(): lax.all_gather(west_part, ('face', 'row'), axis=0, tiled=True)  58.4 us
  transfers between devices with their start and end apart: 4, of which 4 were waited for; matrix products, arithmetic and copies ran while one was open for 2% of the time, Pallas kernels for 0%

commit v1 on v0

v1 whole, which is shorter than its diff:
```python
import functools

import jax
import jax.numpy as jnp
from jax import lax
from jax.experimental import pallas as pl
from jax.experimental.pallas import tpu as pltpu
from jax.sharding import PartitionSpec as P

MESH = pl.DeviceIdType.MESH
BF16 = jnp.bfloat16
F32 = jnp.float32
SNAPS = 2048
ROWS = 24
SIDE = 48
BLK = 512
LANE = 128
GRAM_SCALE = 1.0 / (32 * 48 * 48)


def face_of(y, x, c):
    return (y * 4 + x) * 2 + c


def copy_to(src, dst, send_sem, recv_sem, device):
    return pltpu.make_async_remote_copy(
        src_ref=src,
        dst_ref=dst,
        send_sem=send_sem,
        recv_sem=recv_sem,
        device_id=device,
        device_id_type=MESH,
    )


def wait_bytes(ref, sem):
    pltpu.make_async_copy(ref, ref, sem).wait()


def kernel(
    links,
    turns,
    field,
    mask,
    area,
    anom,
    gram,
    tmp,
    lines,
    first,
    inner,
    gathered,
    chosen,
    arrived,
    east,
    north,
    slope,
    sums,
    own,
    end_in,
    mid_in,
    far_in,
    keep,
    give,
    take,
    mixed_d,
    mixed_t,
    red_d,
    red_t,
    piece_d,
    piece_t,
    fin_d,
    fin_t,
    halo_s,
    halo_r,
    sum_s,
    sum_r,
    str_s,
    end_r,
    mid_r,
    far_r,
    pair_s,
    pair_r,
    dir_s,
    dir_r,
    tra_s,
    tra_r,
    fin_s,
    fin_r,
):
    s = lax.axis_index("snapshot")
    f = lax.axis_index("face")
    r = lax.axis_index("row")
    chip = f // 2
    c = f % 2
    y = chip // 4
    x = chip % 4
    side = s // 2
    is_mid = (s == 1) | (s == 2)
    my_mid = 1 + side
    my_end = 3 * side
    other_mid = 2 - side
    other_end = 3 - 3 * side
    hfar = side
    hnear = 1 - side

    barrier = pltpu.get_barrier_semaphore()

    def greet(device):
        pl.semaphore_signal(barrier, inc=1, device_id=device, device_id_type=MESH)

    greet((s, f, 1 - r))
    greet((s, face_of(y, x, 1 - c), r))

    def greet_chip(step, carry):
        greet((s, 2 * ((chip + step) % 16) + c, r))
        return carry

    lax.fori_loop(1, 16, greet_chip, 0)

    def greet_plane(step, carry):
        greet(((s + step) % 4, f, r))
        greet(((s + step) % 4, f, 1 - r))
        return carry

    lax.fori_loop(1, 4, greet_plane, 0)
    pl.semaphore_wait(barrier, 23)

    tmp[...] = jnp.zeros_like(tmp)
    for i in range(ROWS):
        tmp[i : i + 1, :] = field[0, i, 0:16, :].astype(F32)[0:1]
    lines[r] = tmp[...].astype(BF16)
    row0 = field[0, 0].astype(F32)
    zpad = jnp.zeros((8, BLK), F32)
    for h in range(2):
        first[h] = jnp.concatenate([row0[24 * h : 24 * h + 24], zpad], axis=0).astype(BF16)

    @pl.when(r == 0)
    def _():
        lines[2:4] = first[...]
        a = copy_to(lines.at[0], lines.at[0], halo_s.at[0], halo_r.at[0], (s, f, 1))
        b = copy_to(first, lines.at[2:4], halo_s.at[1], halo_r.at[1], (s, f, 1))
        a.start()
        b.start()
        copy_to(lines.at[1], lines.at[1], halo_s.at[0], halo_r.at[0], (s, f, 1)).wait_recv()
        copy_to(first, inner, halo_s.at[1], halo_r.at[1], (s, f, 1)).wait_recv()
        a.wait_send()
        b.wait_send()

    @pl.when(r == 1)
    def _():
        inner[...] = first[...]
        a = copy_to(lines.at[1], lines.at[1], halo_s.at[0], halo_r.at[0], (s, f, 0))
        b = copy_to(first, inner, halo_s.at[1], halo_r.at[1], (s, f, 0))
        a.start()
        b.start()
        copy_to(lines.at[0], lines.at[0], halo_s.at[0], halo_r.at[0], (s, f, 0)).wait_recv()
        copy_to(first, lines.at[2:4], halo_s.at[1], halo_r.at[1], (s, f, 0)).wait_recv()
        a.wait_send()
        b.wait_send()

    gathered[c, y] = lines[...]
    ysends = []
    for step in range(1, 4):
        yd = (y + step) % 4
        d = copy_to(
            lines, gathered.at[c, y], halo_s.at[1 + step], halo_r.at[1 + step], (s, face_of(yd, x, c), r)
        )
        d.start()
        ysends.append(d)
    for step in range(1, 4):
        ysrc = (y + 4 - step) % 4
        copy_to(
            lines, gathered.at[c, ysrc], halo_s.at[1 + step], halo_r.at[1 + step], (s, f, r)
        ).wait_recv()
    d = copy_to(gathered.at[c], gathered.at[c], halo_s.at[5], halo_r.at[5], (s, face_of(y, x, 1 - c), r))
    d.start()
    copy_to(
        gathered.at[1 - c], gathered.at[1 - c], halo_s.at[5], halo_r.at[5], (s, f, r)
    ).wait_recv()

    def request(tile, m):
        k = 0 if m == 0 else 1
        j = r if m == 0 else m - 1
        u = links[tile, k]
        turn = turns[tile, k]
        odd = turn % 2
        half = j + odd - 2 * j * odd
        return u // 8, (u // 2) % 4, u % 2, 2 * (turn // 2) + half, odd

    for xd in range(4):
        tile = face_of(y, xd, c)
        for m in range(3):
            uy, ux, uc, q, odd = request(tile, m)
            chosen[xd, m] = gathered[uc, uy, q]

    arrived[x] = chosen[x]
    xsends = []
    for step in range(1, 4):
        xd = (x + step) % 4
        e = copy_to(
            chosen.at[xd], arrived.at[x], halo_s.at[5 + step], halo_r.at[5 + step], (s, face_of(y, xd, c), r)
        )
        e.start()
        xsends.append(e)
    for step in range(1, 4):
        xsrc = (x + 4 - step) % 4
        copy_to(
            chosen.at[x], arrived.at[xsrc], halo_s.at[5 + step], halo_r.at[5 + step], (s, f, r)
        ).wait_recv()
    for e in ysends + [d] + xsends:
        e.wait_send()

    turned = []
    ra = lax.broadcasted_iota(jnp.int32, (32, 32), 0)
    rb = lax.broadcasted_iota(jnp.int32, (32, 32), 1)
    for m in range(3):
        uy, ux, uc, q, odd = request(f, m)
        flip = jnp.where(rb == ra + odd * (23 - 2 * ra), 1.0, 0.0).astype(BF16)
        turned.append(jnp.dot(flip, arrived[ux, m], preferred_element_type=F32))
    east[...] = turned[0]
    at_top = jnp.full((24, BLK), r, jnp.int32) == 1
    north[0:24, :] = jnp.where(at_top, turned[1][0:24], inner[0].astype(F32)[0:24])
    north[24:48, :] = jnp.where(at_top, turned[2][0:24], inner[1].astype(F32)[0:24])

    eye = lax.broadcasted_iota(jnp.int32, (SIDE, SIDE), 0) == lax.broadcasted_iota(jnp.int32, (SIDE, SIDE), 1)
    last = lax.broadcasted_iota(jnp.int32, (SIDE, BLK), 0) == SIDE - 1
    lane = lax.broadcasted_iota(jnp.int32, (SIDE, LANE), 1)

    def column(row):
        return jnp.sum(jnp.where(eye, row, 0.0), axis=1, keepdims=True)

    def slope_row(i, acc):
        here = field[0, i].astype(F32)
        above = field[0, jnp.minimum(i + 1, ROWS - 1)].astype(F32)
        above = jnp.where(jnp.full((SIDE, BLK), i, jnp.int32) == ROWS - 1, north[...], above)
        right = jnp.where(last, east[pl.ds(i, 1), :], pltpu.roll(here, SIDE - 1, 0))
        gc = right - here
        gr = above - here
        inv = column(1.0 / area[0, pl.ds(i, 1), :])
        value = jnp.sqrt(1.0 + (gc * gc + gr * gr) * inv)
        slope[i] = value
        return jnp.where(lane == i, jnp.sum(value, axis=1, keepdims=True), acc)

    sums[s] = lax.fori_loop(0, ROWS, slope_row, jnp.zeros((SIDE, LANE), F32))
    psends = []
    for step in range(1, 4):
        e = copy_to(sums.at[s], sums.at[s], sum_s.at[step], sum_r.at[step], ((s + step) % 4, f, r))
        e.start()
        psends.append(e)
    for step in range(1, 4):
        src = (s + 4 - step) % 4
        copy_to(sums.at[src], sums.at[src], sum_s.at[step], sum_r.at[step], (s, f, r)).wait_recv()
    mean = (sums[0] + sums[1] + sums[2] + sums[3]) * (1.0 / SNAPS)
    for e in psends:
        e.wait_send()

    def anomaly_row(i, carry):
        m = jnp.sum(jnp.where(lane == i, mean, 0.0), axis=1, keepdims=True)
        w = column(jnp.sqrt(area[0, pl.ds(i, 1), :]) * mask[0, pl.ds(i, 1), :].astype(F32))
        value = (w * (slope[i] - m)).astype(BF16)
        anom[0, i] = value
        half = i // 12
        for k in range(4):
            own[k, half, i - 12 * half] = value[:, LANE * k : LANE * k + LANE]
        return carry

    lax.fori_loop(0, ROWS, anomaly_row, 0)

    def plane(mid):
        nb = 4 if mid else 3
        nt = nb - 1
        fmid = (other_mid, f, r)
        tend = (my_end, f, r)
        tmid = (my_mid, f, r)

        def chunk_of(k):
            return (k + y) % 4

        def send_own(k):
            kk = chunk_of(k)
            if mid:
                copy_to(own.at[kk, hfar], mid_in.at[kk], str_s.at[0, kk], mid_r.at[kk], fmid).start()
            else:
                copy_to(own.at[kk, hfar], end_in.at[kk, hfar], str_s.at[0, kk], end_r.at[kk, hfar], tmid).start()
                copy_to(own.at[kk, hnear], end_in.at[kk, hnear], str_s.at[1, kk], end_r.at[kk, hnear], tmid).start()

        def product(chunk, rows, acc):
            v = lax.dot_general(
                chunk.reshape(576, LANE),
                rows.reshape(576, BLK),
                (((0,), (0,)), ((), ())),
                preferred_element_type=F32,
            )
            return v if acc is None else acc + v

        def spread(k):
            kk = chunk_of(k)
            wait_bytes(take.at[k, 0 : 16 * (nb + nt)], pair_r.at[k])
            for b in range(nb):
                v = keep[k, 16 * b : 16 * b + 16] + take[k, 16 * b : 16 * b + 16].astype(F32)
                mixed_d[k, :, b] = v.astype(BF16)
            for b in range(nt):
                o = 16 * (nb + b)
                v = keep[k, o : o + 16] + take[k, o : o + 16].astype(F32)
                mixed_t[k, :, 4 * b : 4 * b + 4] = v.astype(BF16).reshape(4, 4, 16, LANE)
            red_d[kk, chip, 0:nb] = mixed_d[k, chip, 0:nb]

            def send_direct(step, carry):
                to = (chip + step) % 16
                copy_to(
                    mixed_d.at[k, to, 0:nb],
                    red_d.at[kk, chip, 0:nb],
                    dir_s.at[k],
                    dir_r.at[k],
                    (s, 2 * to + c, r),
                ).start()
                return carry

            lax.fori_loop(1, 16, send_direct, 0)

            def send_turned(step, carry):
                xd = (x + step) % 4
                copy_to(
                    mixed_t.at[k, xd, 0 : 4 * nt],
                    red_t.at[chip, 0 : 4 * nt],
                    tra_s.at[k],
                    tra_r.at[k],
                    (s, face_of(kk, xd, c), r),
                ).start()
                return carry

            lax.fori_loop(1, 4, send_turned, 0)

            @pl.when(k == 0)
            def _():
                red_t[chip, 0 : 4 * nt] = mixed_t[k, x, 0 : 4 * nt]

            @pl.when(k != 0)
            def _():
                send_turned(0, 0)

        send_own(0)
        send_own(1)

        def step(k, carry):
            kk = chunk_of(k)

            @pl.when(k < 2)
            def _():
                send_own(k + 2)

            if mid:
                ef = copy_to(end_in.at[kk, hfar], far_in.at[kk], str_s.at[1, kk], end_r.at[kk, hfar], fmid)
                ef.wait_recv()
                copy_to(end_in.at[kk, hfar], far_in.at[kk], str_s.at[1, kk], far_r.at[kk], fmid).start()
            wait_bytes(mid_in.at[kk], mid_r.at[kk])
            if mid:
                copy_to(mid_in.at[kk], mid_in.at[kk], str_s.at[2, kk], mid_r.at[kk], tend).start()
            wait_bytes(far_in.at[kk], far_r.at[kk])
            if mid:
                copy_to(far_in.at[kk], far_in.at[kk], str_s.at[3, kk], far_r.at[kk], tend).start()
                wait_bytes(end_in.at[kk, hnear], end_r.at[kk, hnear])
            near_rows = anom[0, pl.ds(12 * hnear, 12)]
            far_rows = anom[0, pl.ds(12 * hfar, 12)]
            results = [
                product(own[kk, hfar], far_rows, product(own[kk, hnear], near_rows, None)),
                product(mid_in[kk], near_rows, None),
                product(far_in[kk], near_rows, None),
            ]
            if mid:
                results.append(
                    product(end_in[kk, hfar], far_rows, product(end_in[kk, hnear], near_rows, None))
                )
            for b in range(nb):
                pt = results[b]
                p = jnp.transpose(pt).reshape(16, 2, 16, LANE)
                for core in range(2):
                    @pl.when(c == core)
                    def _():
                        keep[k, 16 * b : 16 * b + 16] = p[:, core]
                        give[k, 16 * b : 16 * b + 16] = p[:, 1 - core].astype(BF16)
                if b > 0:
                    o = 16 * (nb + b - 1)
                    pq = pt.reshape(4, 2, 16, BLK)
                    for core in range(2):
                        @pl.when(c == core)
                        def _():
                            for xd in range(4):
                                for l in range(4):
                                    ls = slice(LANE * l, LANE * l + LANE)
                                    keep[k, o + 4 * xd + l] = pq[xd, core, :, ls]
                                    give[k, o + 4 * xd + l] = pq[xd, 1 - core, :, ls].astype(BF16)
            copy_to(
                give.at[k, 0 : 16 * (nb + nt)],
                take.at[k, 0 : 16 * (nb + nt)],
                pair_s.at[k],
                pair_r.at[k],
                (s, face_of(y, x, 1 - c), r),
            ).start()

            @pl.when(k > 0)
            def _():
                spread(k - 1)

            return carry

        lax.fori_loop(0, 4, step, 0)
        spread(3)

        for k in range(4):
            wait_bytes(red_d.at[0, 0:15, 0:nb], dir_r.at[k])
            wait_bytes(red_t.at[0 : (3 if k == 0 else 4), 0 : 4 * nt], tra_r.at[k])

        for k in range(4):
            ls = slice(LANE * k, LANE * k + LANE)

            def add_direct(i, acc):
                return acc + red_d[k, i, 0:nb].astype(F32)

            total = lax.fori_loop(1, 16, add_direct, red_d[k, 0, 0:nb].astype(F32))
            for b in range(nb):
                piece_d[0, b, :, ls] = total[b, 0:8]
                piece_d[1, b, :, ls] = total[b, 8:16]
        def add_turned(i, acc):
            return acc + red_t[i, 0 : 4 * nt].astype(F32)

        total = lax.fori_loop(1, 16, add_turned, red_t[0, 0 : 4 * nt].astype(F32))
        for b in range(nt):
            for l in range(4):
                ls = slice(LANE * l, LANE * l + LANE)
                piece_t[0, b, :, ls] = total[4 * b + l, 0:8]
                piece_t[1, b, :, ls] = total[4 * b + l, 8:16]

        ends = []
        e = copy_to(piece_d.at[1 - r, 0:nb], fin_d.at[0:nb], fin_s.at[0], fin_r.at[0], (s, f, 1 - r))
        e.start()
        ends.append(e)
        others = [other_mid, other_end] + ([my_end] if mid else [])
        for b in range(nt):
            for q in range(2):
                e = copy_to(
                    piece_t.at[q, b],
                    fin_t.at[s, r],
                    fin_s.at[1 + 2 * b + q],
                    fin_r.at[1 + 2 * s + r],
                    (others[b], f, q),
                )
                e.start()
                ends.append(e)
        wait_bytes(fin_d.at[0:nb], fin_r.at[0])
        sources = [other_mid, other_end] + ([] if mid else [my_mid])
        for p in sources:
            for q in range(2):
                wait_bytes(fin_t.at[p, q], fin_r.at[1 + 2 * p + q])

        def put(block, value):
            gram[:, pl.ds(pl.multiple_of(block * BLK, BLK), BLK)] = value * GRAM_SCALE

        put(s, piece_d[r, 0] + fin_d[0])
        put(other_mid, piece_d[r, 1] + fin_d[1] + (fin_t[other_mid, 0] + fin_t[other_mid, 1]))
        put(other_end, piece_d[r, 2] + fin_d[2] + (fin_t[other_end, 0] + fin_t[other_end, 1]))
        if mid:
            put(my_end, piece_d[r, 3] + fin_d[3])
        else:
            put(my_mid, fin_t[my_mid, 0] + fin_t[my_mid, 1])

        for e in ends:
            e.wait_send()
        for k in range(4):
            wait_bytes(own.at[0, 0], str_s.at[0, k])
            wait_bytes(own.at[0, 0], str_s.at[1, k])
            if mid:
                wait_bytes(own.at[0, 0], str_s.at[2, k])
                wait_bytes(own.at[0, 0], str_s.at[3, k])
            wait_bytes(give.at[k, 0 : 16 * (nb + nt)], pair_s.at[k])
            wait_bytes(mixed_d.at[0, 0:15, 0:nb], dir_s.at[k])
            wait_bytes(red_t.at[0 : (3 if k == 0 else 4), 0 : 4 * nt], tra_s.at[k])

    @pl.when(is_mid)
    def _():
        plane(True)

    @pl.when(jnp.logical_not(is_mid))
    def _():
        plane(False)


def per_device(surface_field, ocean_mask, cell_area, tile_links, edge_turns):
    vmem = pl.BlockSpec(memory_space=pltpu.VMEM)
    smem = pl.BlockSpec(memory_space=pltpu.SMEM)
    dma = pltpu.SemaphoreType.DMA
    return pl.pallas_call(
        kernel,
        out_shape=(
            jax.ShapeDtypeStruct((1, ROWS, SIDE, BLK), BF16),
            jax.ShapeDtypeStruct((8, SNAPS), F32),
        ),
        in_specs=[smem, smem, vmem, vmem, vmem],
        out_specs=(vmem, vmem),
        scratch_shapes=[
            pltpu.VMEM((32, BLK), F32),
            pltpu.VMEM((4, 32, BLK), BF16),
            pltpu.VMEM((2, 32, BLK), BF16),
            pltpu.VMEM((2, 32, BLK), BF16),
            pltpu.VMEM((2, 4, 4, 32, BLK), BF16),
            pltpu.VMEM((4, 3, 32, BLK), BF16),
            pltpu.VMEM((4, 3, 32, BLK), BF16),
            pltpu.VMEM((32, BLK), F32),
            pltpu.VMEM((SIDE, BLK), F32),
            pltpu.VMEM((ROWS, SIDE, BLK), F32),
            pltpu.VMEM((4, SIDE, LANE), F32),
            pltpu.VMEM((4, 2, 12, SIDE, LANE), BF16),
            pltpu.VMEM((4, 2, 12, SIDE, LANE), BF16),
            pltpu.VMEM((4, 12, SIDE, LANE), BF16),
            pltpu.VMEM((4, 12, SIDE, LANE), BF16),
            pltpu.VMEM((4, 112, 16, LANE), F32),
            pltpu.VMEM((4, 112, 16, LANE), BF16),
            pltpu.VMEM((4, 112, 16, LANE), BF16),
            pltpu.VMEM((4, 16, 4, 16, LANE), BF16),
            pltpu.VMEM((4, 4, 12, 16, LANE), BF16),
            pltpu.VMEM((4, 16, 4, 16, LANE), BF16),
            pltpu.VMEM((16, 12, 16, LANE), BF16),
            pltpu.VMEM((2, 4, 8, BLK), F32),
            pltpu.VMEM((2, 3, 8, BLK), F32),
            pltpu.VMEM((4, 8, BLK), F32),
            pltpu.VMEM((4, 2, 8, BLK), F32),
            dma((9,)),
            dma((9,)),
            dma((4,)),
            dma((4,)),
            dma((4, 4)),
            dma((4, 2)),
            dma((4,)),
            dma((4,)),
            dma((4,)),
            dma((4,)),
            dma((4,)),
            dma((4,)),
            dma((4,)),
            dma((4,)),
            dma((7,)),
            dma((9,)),
        ],
        compiler_params=pltpu.CompilerParams(
            collective_id=0, has_side_effects=True, vmem_limit_bytes=56 * 1024 * 1024
        ),
        name="slope_gram",
    )(tile_links, edge_turns, surface_field, ocean_mask, cell_area)


def solution(mesh):
    placed = (
        P("face", "row", None, "snapshot"),
        P("face", "row", None),
        P("face", "row", None),
        P(),
        P(),
    )
    return jax.shard_map(
        per_device,
        mesh=mesh,
        in_specs=placed,
        out_specs=(P("face", "row", None, "snapshot"), P(("snapshot", "face", "row"), None)),
        check_vma=False,
    )
```

time: 1150 us -> 109 us (0.09); the launches traced: 1130 us -> 109 us
  waiting for transfers between devices: 1030 us -> 0 us
  Pallas kernels: 0 us -> 102 us
  other arithmetic: 24.6 us -> 0 us
  local copies, waits for them, and re-layouts: 29.4 us -> 5.76 us
  between operations: 21.2 us -> 0.65 us
  blocking collectives: 17.6 us -> 0 us
    psum x1 -> x0, waiting for transfers between devices: 794 us -> none  [per_device(): full_gram = lax.psum(product * gram_scale, ('face', 'row'))]
    all_gather x3 -> x0, waiting for transfers between devices: 233 us -> none  [the longest x1 88.9 us: per_device(): gathered = lax.all_gather(ocean_points, 'snapshot', axis=1, tiled=True)]
    pallas_call x0 -> x1, Pallas kernels: none -> 102 us  [per_device(): pl.pallas_call(kernel, out_shape=(jax.ShapeDtypeStruct((1, ROWS, SIDE, BL...]
    psum x1 -> x0, blocking collectives: 17.6 us -> none  [per_device(): column_sum = lax.psum(jnp.sum(slope_norm, axis=-1), 'snapshot')]
    convert_element_type x6 -> x0, other arithmetic: 13.8 us -> none  [the longest x2 8.16 us: per_device(): (weighting[:, :, None] * (slope_norm - column_mean[:, :, None])).astype(j...]
  transfers between devices with their start and end apart: 4 -> 0, of which waited for: 4 -> 0; matrix products, arithmetic and copies ran while one was open for 2% -> 0% of each run, Pallas kernels for 0% -> 0%
where the time goes in v1:
time: 109 us
  Pallas kernels  102 us (94%)
  local copies, waits for them, and re-layouts  5.76 us (5%)
    pallas_call x1, Pallas kernels, per_device(): pl.pallas_call(kernel, out_shape=(jax.ShapeDtypeStruct((1, ROWS, SIDE, BL...  102 us
    unnamed x6, local copies, waits for them, and re-layouts  5.76 us

profile of v1, /device:TPU:8, one launch (start us, length us, event | category | flops | bytes accessed | tf_op | source)
XLA Modules:
  0.0 108.5 jit_solution(5836095062999349779)
XLA Ops:
  0.6 1.4 %copy.7.links = s32[32,2]{1,0:T(8,128)} copy(s32[32,2]{0,1:T(2,128)} %param.8) | data formatting | bytes 512 | tf_op args[3]
  2.0 1.4 %copy.8.turns = s32[32,2]{1,0:T(8,128)} copy(s32[32,2]{0,1:T(2,128)} %param.9) | data formatting | bytes 512 | tf_op args[4]
  3.4 102.1 %slope_gram.1 = (bf16[1,24,48,512]{3,2,1,0:T(8,128)(2,1)}, f32[8,2048]{1,0:T(8,128)}) custom-call(s32[32,2]{1,0:T(8,128)} %copy.7.links, s32[32,2]{1,0:T(8,128)} %copy.8.turns, bf16[1,24,48,512]{3,2,1,0:T(8,128)(2,1)} %field.1, s32[1,24,48]{2,1,0:T(8,128)} %mask.1, f32[1,24,48]{2,1,0:T(8,128)} %area.1), custom_call_target="tpu_custom_call" | custom-call | tf_op jit(solution)/shard_map/slope_gram/pallas_call | solution.py:493
  105.5 0.0 copy-start
  105.5 2.4 %copy.11 = bf16[1,24,48,512]{3,2,1,0:T(8,128)(2,1)} copy(bf16[1,24,48,512]{3,2,1,0:T(8,128)(2,1)} %get-tuple-element.4) | data formatting | bytes 2359296
  107.9 0.0 copy-done
  107.9 0.6 copy.12
Async XLA Ops:
  105.5 2.4 %copy-start = (f32[8,2048]{1,0:T(8,128)S(1)}, f32[8,2048]{1,0:T(8,128)}, u32[]{:S(2)}) copy-start(f32[8,2048]{1,0:T(8,128)} %get-tuple-element.5) | copy-start | bytes 196612

commit v2 on v1

v2 whole, which is shorter than its diff:
```python
import functools

import jax
import jax.numpy as jnp
from jax import lax
from jax.experimental import pallas as pl
from jax.experimental.pallas import tpu as pltpu
from jax.sharding import PartitionSpec as P

MESH = pl.DeviceIdType.MESH
BF16 = jnp.bfloat16
F32 = jnp.float32
SNAPS = 2048
ROWS = 24
SIDE = 48
BLK = 512
LANE = 128
GRAM_SCALE = 1.0 / (32 * 48 * 48)


def face_of(y, x, c):
    return (y * 4 + x) * 2 + c


def copy_to(src, dst, send_sem, recv_sem, device):
    return pltpu.make_async_remote_copy(
        src_ref=src,
        dst_ref=dst,
        send_sem=send_sem,
        recv_sem=recv_sem,
        device_id=device,
        device_id_type=MESH,
    )


def wait_bytes(ref, sem):
    pltpu.make_async_copy(ref, ref, sem).wait()


def kernel(
    links,
    field,
    mask,
    area,
    anom,
    gram,
    line_f,
    edge_f,
    halfw,
    otherw,
    others,
    lines,
    gathered,
    chosen,
    arrived,
    east,
    north,
    slope,
    slope_e,
    cells,
    sums,
    sums_e,
    shift,
    level,
    own,
    end_in,
    mid_in,
    far_in,
    edge_rows,
    edge_own,
    edge_end,
    edge_mid,
    edge_far,
    acc,
    keep,
    give,
    take,
    mixed_d,
    mixed_t,
    red_d,
    red_t,
    piece_d,
    piece_n,
    piece_t,
    mixed_n,
    fin_d,
    fin_n,
    fin_t,
    halo_s,
    halo_r,
    sum_s,
    sum_r,
    str_s,
    end_r,
    mid_r,
    far_r,
    edg_s,
    edg_r,
    pair_s,
    pair_r,
    dir_s,
    dir_r,
    tra_s,
    tra_r,
    fin_s,
    fin_r,
):
    s = lax.axis_index("snapshot")
    f = lax.axis_index("face")
    r = lax.axis_index("row")
    chip = f // 2
    c = f % 2
    y = chip // 4
    x = chip % 4
    side = s // 2
    is_mid = (s == 1) | (s == 2)
    my_mid = 1 + side
    my_end = 3 * side
    other_mid = 2 - side
    other_end = 3 - 3 * side
    hfar = side
    hnear = 1 - side
    at_mid = (other_mid, f, r)
    at_end = (my_end, f, r)
    at_my_mid = (my_mid, f, r)
    at_core = (s, face_of(y, x, 1 - c), r)

    def on_mid(do):
        pl.when(is_mid)(do)

    def on_end(do):
        pl.when(jnp.logical_not(is_mid))(do)

    def chunk_of(k):
        return (k + y) % 4

    barrier = pltpu.get_barrier_semaphore()

    def greet(device):
        pl.semaphore_signal(barrier, inc=1, device_id=device, device_id_type=MESH)

    greet((s, f, 1 - r))
    greet(at_core)

    def greet_chip(step, carry):
        greet((s, 2 * ((chip + step) % 16) + c, r))
        return carry

    lax.fori_loop(1, 16, greet_chip, 0)

    def greet_plane(step, carry):
        greet(((s + step) % 4, f, r))
        greet(((s + step) % 4, f, 1 - r))
        return carry

    lax.fori_loop(1, 4, greet_plane, 0)

    eye = lax.broadcasted_iota(jnp.int32, (SIDE, SIDE), 0) == lax.broadcasted_iota(jnp.int32, (SIDE, SIDE), 1)
    last = lax.broadcasted_iota(jnp.int32, (SIDE, BLK), 0) == SIDE - 1
    inside = lax.broadcasted_iota(jnp.int32, (SIDE, 1), 0) < SIDE - 1
    lane = lax.broadcasted_iota(jnp.int32, (SIDE, LANE), 1)

    def column(row):
        return jnp.sum(jnp.where(eye, row, 0.0), axis=1, keepdims=True)

    def weight_row(i):
        return jnp.sqrt(area[0, pl.ds(i, 1), :]) * mask[0, pl.ds(i, 1), :].astype(F32)

    def steepness(gc, gr, inv):
        return jnp.sqrt(1.0 + (gc * gc + gr * gr) * inv)

    def inner_row(i, carry):
        total, weights = carry
        here = field[0, i].astype(F32)
        above = field[0, i + 1].astype(F32)
        value = steepness(pltpu.roll(here, SIDE - 1, 0) - here, above - here, column(1.0 / area[0, pl.ds(i, 1), :]))
        slope[i] = value
        sv = jnp.sum(value, axis=1, keepdims=True)
        w = jnp.where(inside, column(weight_row(i)), 0.0)
        out = (w * (value - sv * (1.0 / BLK))).astype(BF16)
        half = i // 11
        for k in range(4):
            own[k, half, i - 11 * half] = out[:, LANE * k : LANE * k + LANE]
        return jnp.where(lane == i, sv, total), jnp.where(lane == i, w, weights)

    zero = jnp.zeros((SIDE, LANE), F32)
    total, weights = lax.fori_loop(0, 22, inner_row, (zero, zero))
    sums[s] = total

    line_f[...] = jnp.zeros_like(line_f)
    for i in range(ROWS):
        line_f[i : i + 1, :] = field[0, i, 0:16, :].astype(F32)[0:1]
        edge_f[i : i + 1, :] = field[0, i, 32:48, :].astype(F32)[15:16]
    halfw[...] = line_f[...].astype(BF16)

    pl.semaphore_wait(barrier, 23)

    other_row = (s, f, 1 - r)
    za = copy_to(halfw, otherw, halo_s.at[0], halo_r.at[0], other_row)
    zb = copy_to(field.at[0, 0], others, halo_s.at[1], halo_r.at[1], other_row)
    za.start()
    zb.start()

    def send_sums(ref, n):
        for step in range(1, 4):
            copy_to(ref.at[s], ref.at[s], sum_s.at[n, step], sum_r.at[n, step], ((s + step) % 4, f, r)).start()

    def wait_sums(ref, n):
        for step in range(1, 4):
            wait_bytes(ref.at[0], sum_r.at[n, step])
        for step in range(1, 4):
            wait_bytes(ref.at[0], sum_s.at[n, step])

    def send_own(k):
        kk = chunk_of(k)

        @on_mid
        def _():
            copy_to(own.at[kk, hfar], mid_in.at[kk], str_s.at[0, kk], mid_r.at[kk], at_mid).start()

        @on_end
        def _():
            copy_to(own.at[kk, hfar], end_in.at[kk, hfar], str_s.at[0, kk], end_r.at[kk, hfar], at_my_mid).start()
            copy_to(own.at[kk, hnear], end_in.at[kk, hnear], str_s.at[1, kk], end_r.at[kk, hnear], at_my_mid).start()

    def pass_end(k):
        @on_mid
        def _():
            kk = chunk_of(k)
            wait_bytes(end_in.at[kk, hfar], end_r.at[kk, hfar])
            copy_to(end_in.at[kk, hfar], far_in.at[kk], str_s.at[1, kk], far_r.at[kk], at_mid).start()

    def pass_mid(k):
        @on_mid
        def _():
            kk = chunk_of(k)
            wait_bytes(mid_in.at[kk], mid_r.at[kk])
            copy_to(mid_in.at[kk], mid_in.at[kk], str_s.at[2, kk], mid_r.at[kk], at_end).start()

    def pass_far(k):
        @on_mid
        def _():
            kk = chunk_of(k)
            wait_bytes(far_in.at[kk], far_r.at[kk])
            copy_to(far_in.at[kk], far_in.at[kk], str_s.at[3, kk], far_r.at[kk], at_end).start()

    send_sums(sums, 0)
    send_own(0)
    send_own(1)

    za.wait_recv()
    zb.wait_recv()
    low = jnp.full((ROWS, BLK), r, jnp.int32) == 0
    wa = line_f[0:ROWS]
    wb = otherw[...].astype(F32)[0:ROWS]
    west = jnp.concatenate([jnp.where(low, wa, wb), jnp.where(low, wb, wa)], axis=0).astype(BF16)
    south = jnp.where(
        jnp.full((SIDE, BLK), r, jnp.int32) == 0, field[0, 0].astype(F32), others[...].astype(F32)
    ).astype(BF16)

    def place(p, a, b):
        return face_of(a, b, c) if p == 0 else face_of(b, a, c)

    here_on = [(y, x), (x, y)]
    for p in range(2):
        a, b = here_on[p]
        ls = slice(256 * p, 256 * p + 256)
        lines[p, 0] = west[:, ls]
        lines[p, 1] = south[:, ls]
        gathered[p, c, a, 0] = west[:, ls]
        gathered[p, c, a, 1] = south[:, ls]
        for step in range(1, 4):
            n = 1 + 3 * p + step
            copy_to(
                lines.at[p], gathered.at[p, c, a], halo_s.at[n], halo_r.at[n], (s, place(p, (a + step) % 4, b), r)
            ).start()

    wait_sums(sums, 0)
    mean = (sums[0] + sums[1] + sums[2] + sums[3]) * (1.0 / SNAPS)
    sources = [other_mid, other_end, my_end]
    deltas = [weights * (sums[p] * (1.0 / BLK) - mean) for p in sources]

    def pick(matrix, i):
        return jnp.sum(jnp.where(lane == i, matrix, 0.0), axis=1, keepdims=True)

    def inner_anomaly(i, carry):
        w = column(weight_row(i))
        anom[0, i] = (w * (slope[i] - pick(mean, i))).astype(BF16)
        for b in range(3):
            shift[b, i] = jnp.broadcast_to(pick(deltas[b], i), (SIDE, LANE)).astype(BF16)
        return carry

    lax.fori_loop(0, 22, inner_anomaly, 0)
    pass_end(0)
    pass_mid(0)

    for p in range(2):
        a, b = here_on[p]
        for step in range(1, 4):
            wait_bytes(lines.at[p], halo_r.at[1 + 3 * p + step])
        copy_to(gathered.at[p, c], gathered.at[p, c], halo_s.at[8 + p], halo_r.at[8 + p], at_core).start()
    pass_far(0)

    def request(tile, side_index):
        u = links[2 * tile + side_index]
        turn = links[64 + 2 * tile + side_index]
        return u // 8, (u // 2) % 4, u % 2, turn // 2, turn % 2

    for p in range(2):
        wait_bytes(gathered.at[p, 0], halo_r.at[8 + p])
    for p in range(2):
        a, b = here_on[p]
        for bd in range(4):
            for m in range(2):
                uy, ux, uc, q, odd = request(place(p, a, bd), m)
                chosen[p, bd, m] = gathered[p, uc, uy if p == 0 else ux, q]
        arrived[p, b] = chosen[p, b]
        for step in range(1, 4):
            bd = (b + step) % 4
            n = 9 + 3 * p + step
            to = (s, place(p, a, bd), r)
            copy_to(chosen.at[p, bd, 0], arrived.at[p, b, 0], halo_s.at[n], halo_r.at[n], to).start()

            @pl.when(r == 1)
            def _():
                copy_to(chosen.at[p, bd, 1], arrived.at[p, b, 1], halo_s.at[n + 6], halo_r.at[n + 6], to).start()

    send_own(2)
    pass_end(1)
    pass_mid(1)

    def product(chunk, rows):
        k_size = chunk.shape[0] * chunk.shape[1]
        return lax.dot_general(
            chunk.reshape(k_size, LANE),
            rows.reshape(k_size, BLK),
            (((0,), (0,)), ((), ())),
            preferred_element_type=F32,
        )

    def inner_product(chunk, h):
        return product(chunk[...], anom[0, pl.ds(11 * h, 11)])

    def own_product(kk):
        cols = anom[0, 0:22, :, pl.ds(pl.multiple_of(kk * LANE, LANE), LANE)]
        live = lax.broadcasted_iota(jnp.int32, (22, SIDE, LANE), 1) < SIDE - 1
        cols = jnp.where(live, cols.astype(F32), 0.0).astype(BF16)
        return product(cols, anom[0, 0:22])

    near_inner = pl.ds(11 * hnear, 11)
    level[0] = product(shift[0, near_inner], anom[0, near_inner])
    level[1] = product(shift[1, near_inner], anom[0, near_inner])

    @on_mid
    def _():
        level[2] = product(shift[2], anom[0, 0:22])

    def products(k):
        kk = chunk_of(k)
        acc[0, k] = own_product(kk)

        @on_end
        def _():
            wait_bytes(mid_in.at[kk], mid_r.at[kk])
            wait_bytes(far_in.at[kk], far_r.at[kk])

        acc[1, k] = inner_product(mid_in.at[kk], hnear) + level[0]
        acc[2, k] = inner_product(far_in.at[kk], hnear) + level[1]

        @on_mid
        def _():
            wait_bytes(end_in.at[kk, hnear], end_r.at[kk, hnear])
            acc[3, k] = inner_product(end_in.at[kk, 0], 0) + inner_product(end_in.at[kk, 1], 1) + level[2]

    products(0)

    for p in range(2):
        for step in range(1, 4):
            n = 9 + 3 * p + step
            wait_bytes(arrived.at[0, 0, 0], halo_r.at[n])

            @pl.when(r == 1)
            def _():
                wait_bytes(arrived.at[0, 0, 0], halo_r.at[n + 6])

    row_id = lax.broadcasted_iota(jnp.int32, (SIDE, SIDE), 0)
    col_id = lax.broadcasted_iota(jnp.int32, (SIDE, SIDE), 1)
    for p in range(2):
        ls = slice(256 * p, 256 * p + 256)
        uy, ux, uc, q, odd = request(f, 0)
        cell = row_id[0:32] + 24 * r
        flip = jnp.where(col_id[0:32] == cell + odd * (47 - 2 * cell), 1.0, 0.0).astype(BF16)
        east[:, ls] = jnp.dot(flip, arrived[p, ux if p == 0 else uy, 0], preferred_element_type=F32)

        @pl.when(r == 1)
        def _():
            uy, ux, uc, q, odd = request(f, 1)
            flip = jnp.where(col_id == row_id + odd * (47 - 2 * row_id), 1.0, 0.0).astype(BF16)
            north[:, ls] = jnp.dot(flip, arrived[p, ux if p == 0 else uy, 1], preferred_element_type=F32)

    @pl.when(r == 0)
    def _():
        north[...] = others[...].astype(F32)

    esum = zero
    for h in range(2):
        i = 22 + h
        here = field[0, i].astype(F32)
        above = north[...] if h else field[0, i + 1].astype(F32)
        right = jnp.where(last, east[i : i + 1, :], pltpu.roll(here, SIDE - 1, 0))
        value = steepness(right - here, above - here, column(1.0 / area[0, i : i + 1, :]))
        slope[i] = value
        esum = jnp.where(lane == h, jnp.sum(value, axis=1, keepdims=True), esum)
    ecol = edge_f[...]
    esteep = steepness(
        east[0:ROWS] - ecol, pltpu.roll(ecol, ROWS - 1, 0) - ecol, 1.0 / area[0][:, SIDE - 1 : SIDE]
    )
    slope_e[...] = esteep
    colsum = jnp.concatenate(
        [jnp.sum(esteep, axis=1, keepdims=True), jnp.zeros((SIDE - ROWS, 1), F32)], axis=0
    )
    sums_e[s] = jnp.where(lane == 2, colsum, esum)
    send_sums(sums_e, 1)
    pass_far(1)
    products(1)

    wait_sums(sums_e, 1)
    emean = (sums_e[0] + sums_e[1] + sums_e[2] + sums_e[3]) * (1.0 / SNAPS)
    ew = jnp.sqrt(area[0][:, SIDE - 1 : SIDE]) * mask[0][:, SIDE - 1 : SIDE].astype(F32)
    evalue = ew * (slope_e[...] - pick(emean, 2)[0:ROWS])
    slope_e[...] = evalue
    cells[...] = jnp.zeros_like(cells)
    for h in range(2):
        i = 22 + h
        cells[h, 0:SIDE] = column(weight_row(i)) * (slope[i] - pick(emean, h))
        cells[h, SIDE : SIDE + 11] = evalue[11 * h : 11 * h + 11]
        both = cells[h].astype(BF16)
        anom[0, i] = both[0:SIDE]
        edge_rows[h] = both
        for k in range(4):
            edge_own[h, k] = both[:, LANE * k : LANE * k + LANE]

    @on_mid
    def _():
        copy_to(edge_own.at[hfar], edge_mid, edg_s.at[0], edg_r.at[2], at_mid).start()

    @on_end
    def _():
        copy_to(edge_own.at[hfar], edge_end.at[hfar], edg_s.at[0], edg_r.at[hfar], at_my_mid).start()
        copy_to(edge_own.at[hnear], edge_end.at[hnear], edg_s.at[1], edg_r.at[hnear], at_my_mid).start()

    send_own(3)

    def put_column(i, carry):
        tile = anom[0, i, 32:48].astype(F32)
        at = lax.broadcasted_iota(jnp.int32, (16, BLK), 0) == 15
        anom[0, i, 32:48] = jnp.where(at, slope_e[pl.ds(i, 1), :], tile).astype(BF16)
        return carry

    pass_end(2)
    pass_mid(2)
    pass_far(2)

    @on_mid
    def _():
        wait_bytes(edge_end.at[0], edg_r.at[hfar])
        copy_to(edge_end.at[hfar], edge_far, edg_s.at[1], edg_r.at[3], at_mid).start()
        wait_bytes(edge_mid, edg_r.at[2])
        copy_to(edge_mid, edge_mid, edg_s.at[2], edg_r.at[2], at_end).start()

    products(2)
    pass_end(3)

    @on_mid
    def _():
        wait_bytes(edge_far, edg_r.at[3])
        copy_to(edge_far, edge_far, edg_s.at[3], edg_r.at[3], at_end).start()
        wait_bytes(edge_end.at[0], edg_r.at[hnear])

    @on_end
    def _():
        wait_bytes(edge_mid, edg_r.at[2])
        wait_bytes(edge_far, edg_r.at[3])

    def plane(mid):
        nb = 4 if mid else 3
        nt = nb - 1

        def emit(k):
            kk = chunk_of(k)
            near_edge = edge_rows[hnear]
            extra = [
                product(edge_own[:, kk], edge_rows[...]),
                product(edge_mid[kk][None], near_edge[None]),
                product(edge_far[kk][None], near_edge[None]),
            ]
            if mid:
                extra.append(product(edge_end[:, kk], edge_rows[...]))
            for b in range(nb):
                pt = acc[b, k] + extra[b]
                p = jnp.transpose(pt).reshape(16, 2, 16, LANE)
                for core in range(2):
                    @pl.when(c == core)
                    def _():
                        keep[k, 16 * b : 16 * b + 16] = p[:, core]
                        give[k, 16 * b : 16 * b + 16] = p[:, 1 - core].astype(BF16)
                if b > 0:
                    o = 16 * (nb + b - 1)
                    pq = pt.reshape(4, 2, 16, BLK)
                    for core in range(2):
                        @pl.when(c == core)
                        def _():
                            for xd in range(4):
                                for l in range(4):
                                    ls = slice(LANE * l, LANE * l + LANE)
                                    keep[k, o + 4 * xd + l] = pq[xd, core, :, ls]
                                    give[k, o + 4 * xd + l] = pq[xd, 1 - core, :, ls].astype(BF16)
            copy_to(
                give.at[k, 0 : 16 * (nb + nt)],
                take.at[k, 0 : 16 * (nb + nt)],
                pair_s.at[k],
                pair_r.at[k],
                at_core,
            ).start()

        def spread(k):
            kk = chunk_of(k)
            wait_bytes(take.at[k, 0 : 16 * (nb + nt)], pair_r.at[k])
            for b in range(nb):
                v = keep[k, 16 * b : 16 * b + 16] + take[k, 16 * b : 16 * b + 16].astype(F32)
                mixed_d[k, :, b] = v.astype(BF16)
            for b in range(nt):
                o = 16 * (nb + b)
                v = keep[k, o : o + 16] + take[k, o : o + 16].astype(F32)
                mixed_t[k, :, 4 * b : 4 * b + 4] = v.astype(BF16).reshape(4, 4, 16, LANE)
            red_d[kk, chip, 0:nb] = mixed_d[k, chip, 0:nb]

            def send_direct(step, carry):
                to = (chip + step) % 16
                copy_to(
                    mixed_d.at[k, to, 0:nb],
                    red_d.at[kk, chip, 0:nb],
                    dir_s.at[k],
                    dir_r.at[k],
                    (s, 2 * to + c, r),
                ).start()
                return carry

            lax.fori_loop(1, 16, send_direct, 0)

            def send_turned(step, carry):
                xd = (x + step) % 4
                copy_to(
                    mixed_t.at[k, xd, 0 : 4 * nt],
                    red_t.at[chip, 0 : 4 * nt],
                    tra_s.at[k],
                    tra_r.at[k],
                    (s, face_of(kk, xd, c), r),
                ).start()
                return carry

            lax.fori_loop(1, 4, send_turned, 0)

            @pl.when(k == 0)
            def _():
                red_t[chip, 0 : 4 * nt] = mixed_t[k, x, 0 : 4 * nt]

            @pl.when(k != 0)
            def _():
                send_turned(0, 0)

        def turn(k, carry):
            emit(k)

            @pl.when(k > 0)
            def _():
                spread(k - 1)

            @pl.when(k == 1)
            def _():
                pass_mid(3)
                pass_far(3)

            @pl.when(k == 2)
            def _():
                products(3)

            return carry

        lax.fori_loop(0, 4, turn, 0)
        lax.fori_loop(0, 22, put_column, 0)
        spread(3)

        for k in range(4):
            wait_bytes(red_d.at[0, 0:15, 0:nb], dir_r.at[k])
            wait_bytes(red_t.at[0 : (3 if k == 0 else 4), 0 : 4 * nt], tra_r.at[k])

        for k in range(4):
            ls = slice(LANE * k, LANE * k + LANE)
            ln = slice(LANE * (k % 2), LANE * (k % 2) + LANE)
            rn = slice(8 * (k // 2), 8 * (k // 2) + 8)

            def add_direct(i, acc):
                return acc + red_d[k, i, 0:nb].astype(F32)

            total = lax.fori_loop(1, 16, add_direct, red_d[k, 0, 0:nb].astype(F32))
            for q in range(2):
                piece_d[q, :, ls] = total[0, 8 * q : 8 * q + 8]
                for b in range(nt):
                    piece_n[q, b, rn, ln] = total[1 + b, 8 * q : 8 * q + 8]

        def add_turned(i, acc):
            return acc + red_t[i, 0 : 4 * nt].astype(F32)

        total = lax.fori_loop(1, 16, add_turned, red_t[0, 0 : 4 * nt].astype(F32))
        for b in range(nt):
            for q in range(2):
                rows = slice(8 * q, 8 * q + 8)
                parts = [total[4 * b + l, rows] for l in range(4)]
                top = jnp.concatenate(parts[0:2], axis=1)
                bottom = jnp.concatenate(parts[2:4], axis=1)
                piece_t[q, b] = jnp.concatenate([top, bottom], axis=0).astype(BF16)
        for b in range(nt):
            mixed_n[b] = piece_n[1 - r, b].astype(BF16)

        ends = []
        e = copy_to(piece_d.at[1 - r], fin_d, fin_s.at[0], fin_r.at[0], other_row)
        e.start()
        ends.append(e)
        e = copy_to(mixed_n.at[0:nt], fin_n.at[0:nt], fin_s.at[7], fin_r.at[9], other_row)
        e.start()
        ends.append(e)
        others_of = [other_mid, other_end] + ([my_end] if mid else [])
        for b in range(nt):
            for q in range(2):
                e = copy_to(
                    piece_t.at[q, b],
                    fin_t.at[s, r],
                    fin_s.at[1 + 2 * b + q],
                    fin_r.at[1 + 2 * s + r],
                    (others_of[b], f, q),
                )
                e.start()
                ends.append(e)
        wait_bytes(fin_d, fin_r.at[0])
        wait_bytes(fin_n.at[0:nt], fin_r.at[9])
        sources = [other_mid, other_end] + ([] if mid else [my_mid])
        for p in sources:
            for q in range(2):
                wait_bytes(fin_t.at[p, q], fin_r.at[1 + 2 * p + q])

        def put(block, value):
            gram[:, pl.ds(pl.multiple_of(block * BLK, BLK), BLK)] = value * GRAM_SCALE

        def put_folded(block, value):
            put(block, jnp.concatenate([value[0:8], value[8:16]], axis=1))

        def turned(p):
            return fin_t[p, 0].astype(F32) + fin_t[p, 1].astype(F32)

        def straight(b):
            return piece_n[r, b] + fin_n[b].astype(F32)

        put(s, piece_d[r] + fin_d[...])
        put_folded(other_mid, straight(0) + turned(other_mid))
        put_folded(other_end, straight(1) + turned(other_end))
        if mid:
            put_folded(my_end, straight(2))
        else:
            put_folded(my_mid, turned(my_mid))

        for e in ends:
            e.wait_send()
        for k in range(4):
            wait_bytes(own.at[0, 0], str_s.at[0, k])
            wait_bytes(own.at[0, 0], str_s.at[1, k])
            if mid:
                wait_bytes(own.at[0, 0], str_s.at[2, k])
                wait_bytes(own.at[0, 0], str_s.at[3, k])
            wait_bytes(edge_own.at[0], edg_s.at[k]) if mid or k < 2 else None
            wait_bytes(give.at[k, 0 : 16 * (nb + nt)], pair_s.at[k])
            wait_bytes(mixed_d.at[0, 0:15, 0:nb], dir_s.at[k])
            wait_bytes(red_t.at[0 : (3 if k == 0 else 4), 0 : 4 * nt], tra_s.at[k])

    @on_mid
    def _():
        plane(True)

    @on_end
    def _():
        plane(False)

    za.wait_send()
    zb.wait_send()
    for p in range(2):
        for step in range(1, 4):
            wait_bytes(lines.at[p], halo_s.at[1 + 3 * p + step])
            wait_bytes(arrived.at[0, 0, 0], halo_s.at[9 + 3 * p + step])

            @pl.when(r == 1)
            def _():
                wait_bytes(arrived.at[0, 0, 0], halo_s.at[15 + 3 * p + step])

        wait_bytes(gathered.at[p, 0], halo_s.at[8 + p])


def per_device(surface_field, ocean_mask, cell_area, tile_links, edge_turns):
    vmem = pl.BlockSpec(memory_space=pltpu.VMEM)
    smem = pl.BlockSpec(memory_space=pltpu.SMEM)
    dma = pltpu.SemaphoreType.DMA
    links = jnp.concatenate([tile_links.reshape(-1), edge_turns.reshape(-1)])
    return pl.pallas_call(
        kernel,
        out_shape=(
            jax.ShapeDtypeStruct((1, ROWS, SIDE, BLK), BF16),
            jax.ShapeDtypeStruct((8, SNAPS), F32),
        ),
        in_specs=[smem, vmem, vmem, vmem],
        out_specs=(vmem, vmem),
        scratch_shapes=[
            pltpu.VMEM((32, BLK), F32),
            pltpu.VMEM((ROWS, BLK), F32),
            pltpu.VMEM((32, BLK), BF16),
            pltpu.VMEM((32, BLK), BF16),
            pltpu.VMEM((SIDE, BLK), BF16),
            pltpu.VMEM((2, 2, SIDE, 256), BF16),
            pltpu.VMEM((2, 2, 4, 2, SIDE, 256), BF16),
            pltpu.VMEM((2, 4, 2, SIDE, 256), BF16),
            pltpu.VMEM((2, 4, 2, SIDE, 256), BF16),
            pltpu.VMEM((32, BLK), F32),
            pltpu.VMEM((SIDE, BLK), F32),
            pltpu.VMEM((ROWS, SIDE, BLK), F32),
            pltpu.VMEM((ROWS, BLK), F32),
            pltpu.VMEM((2, 64, BLK), F32),
            pltpu.VMEM((4, SIDE, LANE), F32),
            pltpu.VMEM((4, SIDE, LANE), F32),
            pltpu.VMEM((3, 22, SIDE, LANE), BF16),
            pltpu.VMEM((3, LANE, BLK), F32),
            pltpu.VMEM((4, 2, 11, SIDE, LANE), BF16),
            pltpu.VMEM((4, 2, 11, SIDE, LANE), BF16),
            pltpu.VMEM((4, 11, SIDE, LANE), BF16),
            pltpu.VMEM((4, 11, SIDE, LANE), BF16),
            pltpu.VMEM((2, 64, BLK), BF16),
            pltpu.VMEM((2, 4, 64, LANE), BF16),
            pltpu.VMEM((2, 4, 64, LANE), BF16),
            pltpu.VMEM((4, 64, LANE), BF16),
            pltpu.VMEM((4, 64, LANE), BF16),
            pltpu.VMEM((4, 4, LANE, BLK), F32),
            pltpu.VMEM((4, 112, 16, LANE), F32),
            pltpu.VMEM((4, 112, 16, LANE), BF16),
            pltpu.VMEM((4, 112, 16, LANE), BF16),
            pltpu.VMEM((4, 16, 4, 16, LANE), BF16),
            pltpu.VMEM((4, 4, 12, 16, LANE), BF16),
            pltpu.VMEM((4, 16, 4, 16, LANE), BF16),
            pltpu.VMEM((16, 12, 16, LANE), BF16),
            pltpu.VMEM((2, 8, BLK), F32),
            pltpu.VMEM((2, 3, 16, 256), F32),
            pltpu.VMEM((2, 3, 16, 256), BF16),
            pltpu.VMEM((3, 16, 256), BF16),
            pltpu.VMEM((8, BLK), F32),
            pltpu.VMEM((3, 16, 256), BF16),
            pltpu.VMEM((4, 2, 16, 256), BF16),
            dma((22,)),
            dma((22,)),
            dma((2, 4)),
            dma((2, 4)),
            dma((4, 4)),
            dma((4, 2)),
            dma((4,)),
            dma((4,)),
            dma((4,)),
            dma((4,)),
            dma((4,)),
            dma((4,)),
            dma((4,)),
            dma((4,)),
            dma((4,)),
            dma((4,)),
            dma((8,)),
            dma((10,)),
        ],
        compiler_params=pltpu.CompilerParams(
            collective_id=0, has_side_effects=True, vmem_limit_bytes=56 * 1024 * 1024
        ),
        name="slope_gram",
    )(links, surface_field, ocean_mask, cell_area)


def solution(mesh):
    placed = (
        P("face", "row", None, "snapshot"),
        P("face", "row", None),
        P("face", "row", None),
        P(),
        P(),
    )
    return jax.shard_map(
        per_device,
        mesh=mesh,
        in_specs=placed,
        out_specs=(P("face", "row", None, "snapshot"), P(("snapshot", "face", "row"), None)),
        check_vma=False,
    )
```

time: 109 us -> 90.2 us (0.83)
  Pallas kernels: 102 us -> 84.1 us
    pallas_call x1, Pallas kernels: 102 us -> 84.1 us  [per_device(): pl.pallas_call(kernel, out_shape=(jax.ShapeDtypeStruct((1, ROWS, SIDE, BL...]
    unnamed x6, local copies, waits for them, and re-layouts: 5.76 us -> 4.55 us
where the time goes in v2:
time: 90.2 us; the launch traced here: 90.1 us
  Pallas kernels  84.1 us (93%)
  local copies, waits for them, and re-layouts  4.76 us (5%)
    pallas_call x1, Pallas kernels, per_device(): pl.pallas_call(kernel, out_shape=(jax.ShapeDtypeStruct((1, ROWS, SIDE, BL...  84.1 us
    unnamed x6, local copies, waits for them, and re-layouts  4.55 us

profile of v2, /device:TPU:8, one launch (start us, length us, event | category | flops | bytes accessed | tf_op | source)
XLA Modules:
  0.0 90.1 jit_solution(8538387437436059228)
XLA Ops:
  0.6 0.8 copy.9
  1.4 0.1 reshape.10
  1.5 0.8 copy.10
  2.3 0.1 reshape.11
  2.4 0.6 pad_add_fusion.links
  3.0 84.1 %slope_gram.1 = (bf16[1,24,48,512]{3,2,1,0:T(8,128)(2,1)}, f32[8,2048]{1,0:T(8,128)}) custom-call(s32[128]{0:T(128)} %pad_add_fusion.links, bf16[1,24,48,512]{3,2,1,0:T(8,128)(2,1)} %field.1, s32[1,24,48]{2,1,0:T(8,128)} %mask.1, f32[1,24,48]{2,1,0:T(8,128)} %area.1), custom_call_target="tpu_custom_call" | custom-call | tf_op jit(solution)/shard_map/slope_gram/pallas_call | solution.py:712
  87.0 0.0 copy-start
  87.1 2.4 %copy.13 = bf16[1,24,48,512]{3,2,1,0:T(8,128)(2,1)} copy(bf16[1,24,48,512]{3,2,1,0:T(8,128)(2,1)} %get-tuple-element.4) | data formatting | bytes 2359296
  89.5 0.0 copy-done
  89.5 0.6 copy.14
Async XLA Ops:
  87.0 2.4 %copy-start = (f32[8,2048]{1,0:T(8,128)S(1)}, f32[8,2048]{1,0:T(8,128)}, u32[]{:S(2)}) copy-start(f32[8,2048]{1,0:T(8,128)} %get-tuple-element.5) | copy-start | bytes 196612

commit v3 on v2

--- a/solution.py
+++ b/solution.py
@@ -61,6 +61,7 @@
     sums,
     sums_e,
     shift,
+    shift_e,
     level,
     own,
     end_in,
@@ -79,6 +80,7 @@
     mixed_t,
     red_d,
     red_t,
+    tot,
     piece_d,
     piece_n,
     piece_t,
@@ -211,17 +213,20 @@
         for step in range(1, 4):
             wait_bytes(ref.at[0], sum_s.at[n, step])
 
-    def send_own(k):
-        kk = chunk_of(k)
-
+    def send_mid(k):
         @on_mid
         def _():
+            kk = chunk_of(k)
             copy_to(own.at[kk, hfar], mid_in.at[kk], str_s.at[0, kk], mid_r.at[kk], at_mid).start()
 
+    def send_end(n):
         @on_end
         def _():
-            copy_to(own.at[kk, hfar], end_in.at[kk, hfar], str_s.at[0, kk], end_r.at[kk, hfar], at_my_mid).start()
-            copy_to(own.at[kk, hnear], end_in.at[kk, hnear], str_s.at[1, kk], end_r.at[kk, hnear], at_my_mid).start()
+            if n >= 2:
+                wait_bytes(own.at[0, 0], str_s.at[n % 2, chunk_of(n // 2 - 1)])
+            kk = chunk_of(n // 2)
+            h = hnear if n % 2 else hfar
+            copy_to(own.at[kk, h], end_in.at[kk, h], str_s.at[n % 2, kk], end_r.at[kk, h], at_my_mid).start()
 
     def pass_end(k):
         @on_mid
@@ -245,8 +250,8 @@
             copy_to(far_in.at[kk], far_in.at[kk], str_s.at[3, kk], far_r.at[kk], at_end).start()
 
     send_sums(sums, 0)
-    send_own(0)
-    send_own(1)
+    send_mid(0)
+    send_end(0)
 
     za.wait_recv()
     zb.wait_recv()
@@ -275,6 +280,10 @@
                 lines.at[p], gathered.at[p, c, a], halo_s.at[n], halo_r.at[n], (s, place(p, (a + step) % 4, b), r)
             ).start()
 
+    send_mid(1)
+    pass_mid(0)
+    send_end(1)
+
     wait_sums(sums, 0)
     mean = (sums[0] + sums[1] + sums[2] + sums[3]) * (1.0 / SNAPS)
     sources = [other_mid, other_end, my_end]
@@ -292,14 +301,17 @@
 
     lax.fori_loop(0, 22, inner_anomaly, 0)
     pass_end(0)
-    pass_mid(0)
+    pass_mid(1)
+    send_end(2)
 
     for p in range(2):
         a, b = here_on[p]
         for step in range(1, 4):
             wait_bytes(lines.at[p], halo_r.at[1 + 3 * p + step])
         copy_to(gathered.at[p, c], gathered.at[p, c], halo_s.at[8 + p], halo_r.at[8 + p], at_core).start()
+    send_mid(2)
     pass_far(0)
+    send_end(3)
 
     def request(tile, side_index):
         u = links[2 * tile + side_index]
@@ -325,9 +337,9 @@
             def _():
                 copy_to(chosen.at[p, bd, 1], arrived.at[p, b, 1], halo_s.at[n + 6], halo_r.at[n + 6], to).start()
 
-    send_own(2)
     pass_end(1)
-    pass_mid(1)
+    pass_mid(2)
+    send_end(4)
 
     def product(chunk, rows):
         k_size = chunk.shape[0] * chunk.shape[1]
@@ -364,13 +376,13 @@
             wait_bytes(mid_in.at[kk], mid_r.at[kk])
             wait_bytes(far_in.at[kk], far_r.at[kk])
 
-        acc[1, k] = inner_product(mid_in.at[kk], hnear) + level[0]
-        acc[2, k] = inner_product(far_in.at[kk], hnear) + level[1]
+        acc[1, k] = inner_product(mid_in.at[kk], hnear)
+        acc[2, k] = inner_product(far_in.at[kk], hnear)
 
         @on_mid
         def _():
             wait_bytes(end_in.at[kk, hnear], end_r.at[kk, hnear])
-            acc[3, k] = inner_product(end_in.at[kk, 0], 0) + inner_product(end_in.at[kk, 1], 1) + level[2]
+            acc[3, k] = inner_product(end_in.at[kk, 0], 0) + inner_product(end_in.at[kk, 1], 1)
 
     products(0)
 
@@ -403,6 +415,7 @@
         north[...] = others[...].astype(F32)
 
     esum = zero
+    cells[...] = jnp.zeros_like(cells)
     for h in range(2):
         i = 22 + h
         here = field[0, i].astype(F32)
@@ -410,33 +423,20 @@
         right = jnp.where(last, east[i : i + 1, :], pltpu.roll(here, SIDE - 1, 0))
         value = steepness(right - here, above - here, column(1.0 / area[0, i : i + 1, :]))
         slope[i] = value
-        esum = jnp.where(lane == h, jnp.sum(value, axis=1, keepdims=True), esum)
+        sv = jnp.sum(value, axis=1, keepdims=True)
+        esum = jnp.where(lane == h, sv, esum)
+        cells[h, 0:SIDE] = column(weight_row(i)) * (value - sv * (1.0 / BLK))
     ecol = edge_f[...]
     esteep = steepness(
         east[0:ROWS] - ecol, pltpu.roll(ecol, ROWS - 1, 0) - ecol, 1.0 / area[0][:, SIDE - 1 : SIDE]
     )
     slope_e[...] = esteep
-    colsum = jnp.concatenate(
-        [jnp.sum(esteep, axis=1, keepdims=True), jnp.zeros((SIDE - ROWS, 1), F32)], axis=0
-    )
-    sums_e[s] = jnp.where(lane == 2, colsum, esum)
-    send_sums(sums_e, 1)
-    pass_far(1)
-    products(1)
-
-    wait_sums(sums_e, 1)
-    emean = (sums_e[0] + sums_e[1] + sums_e[2] + sums_e[3]) * (1.0 / SNAPS)
     ew = jnp.sqrt(area[0][:, SIDE - 1 : SIDE]) * mask[0][:, SIDE - 1 : SIDE].astype(F32)
-    evalue = ew * (slope_e[...] - pick(emean, 2)[0:ROWS])
-    slope_e[...] = evalue
-    cells[...] = jnp.zeros_like(cells)
+    esv = jnp.sum(esteep, axis=1, keepdims=True)
+    evalue = ew * (esteep - esv * (1.0 / BLK))
     for h in range(2):
-        i = 22 + h
-        cells[h, 0:SIDE] = column(weight_row(i)) * (slope[i] - pick(emean, h))
         cells[h, SIDE : SIDE + 11] = evalue[11 * h : 11 * h + 11]
         both = cells[h].astype(BF16)
-        anom[0, i] = both[0:SIDE]
-        edge_rows[h] = both
         for k in range(4):
             edge_own[h, k] = both[:, LANE * k : LANE * k + LANE]
 
@@ -449,17 +449,13 @@
         copy_to(edge_own.at[hfar], edge_end.at[hfar], edg_s.at[0], edg_r.at[hfar], at_my_mid).start()
         copy_to(edge_own.at[hnear], edge_end.at[hnear], edg_s.at[1], edg_r.at[hnear], at_my_mid).start()
 
-    send_own(3)
-
-    def put_column(i, carry):
-        tile = anom[0, i, 32:48].astype(F32)
-        at = lax.broadcasted_iota(jnp.int32, (16, BLK), 0) == 15
-        anom[0, i, 32:48] = jnp.where(at, slope_e[pl.ds(i, 1), :], tile).astype(BF16)
-        return carry
-
-    pass_end(2)
-    pass_mid(2)
-    pass_far(2)
+    colsum = jnp.concatenate([esv, jnp.zeros((SIDE - ROWS, 1), F32)], axis=0)
+    sums_e[s] = jnp.where(lane == 2, colsum, esum)
+    send_sums(sums_e, 1)
+    send_mid(3)
+    pass_far(1)
+    send_end(5)
+    products(1)
 
     @on_mid
     def _():
@@ -468,11 +464,36 @@
         wait_bytes(edge_mid, edg_r.at[2])
         copy_to(edge_mid, edge_mid, edg_s.at[2], edg_r.at[2], at_end).start()
 
-    products(2)
-    pass_end(3)
+    wait_sums(sums_e, 1)
+    emean = (sums_e[0] + sums_e[1] + sums_e[2] + sums_e[3]) * (1.0 / SNAPS)
+    evalue = ew * (slope_e[...] - pick(emean, 2)[0:ROWS])
+    slope_e[...] = evalue
+    for h in range(2):
+        i = 22 + h
+        w = column(weight_row(i))
+        cells[h, 0:SIDE] = w * (slope[i] - pick(emean, h))
+        cells[h, SIDE : SIDE + 11] = evalue[11 * h : 11 * h + 11]
+        both = cells[h].astype(BF16)
+        anom[0, i] = both[0:SIDE]
+        edge_rows[h] = both
+    pass_end(2)
+    pass_mid(3)
+    send_end(6)
+    shift_e[...] = jnp.zeros_like(shift_e)
+    for h in range(2):
+        w = column(weight_row(22 + h))
+        for b in range(3):
+            delta = sums_e[sources[b]] * (1.0 / BLK) - emean
+            shift_e[b, h, 0:SIDE] = jnp.broadcast_to(w * pick(delta, h), (SIDE, LANE))
+            rim = ew * pick(delta, 2)[0:ROWS]
+            shift_e[b, h, SIDE : SIDE + 11] = jnp.broadcast_to(rim[11 * h : 11 * h + 11], (11, LANE))
+    near_edge = edge_rows[hnear][None]
+    level[0] += product(shift_e[0, hnear].astype(BF16)[None], near_edge)
+    level[1] += product(shift_e[1, hnear].astype(BF16)[None], near_edge)
 
     @on_mid
     def _():
+        level[2] += product(shift_e[2].astype(BF16), edge_rows[...])
         wait_bytes(edge_far, edg_r.at[3])
         copy_to(edge_far, edge_far, edg_s.at[3], edg_r.at[3], at_end).start()
         wait_bytes(edge_end.at[0], edg_r.at[hnear])
@@ -482,20 +503,26 @@
         wait_bytes(edge_mid, edg_r.at[2])
         wait_bytes(edge_far, edg_r.at[3])
 
+    def put_column(i, carry):
+        tile = anom[0, i, 32:48].astype(F32)
+        at = lax.broadcasted_iota(jnp.int32, (16, BLK), 0) == 15
+        anom[0, i, 32:48] = jnp.where(at, slope_e[pl.ds(i, 1), :], tile).astype(BF16)
+        return carry
+
     def plane(mid):
         nb = 4 if mid else 3
         nt = nb - 1
 
         def emit(k):
             kk = chunk_of(k)
-            near_edge = edge_rows[hnear]
+            cols = pl.ds(pl.multiple_of(kk * LANE, LANE), LANE)
             extra = [
-                product(edge_own[:, kk], edge_rows[...]),
-                product(edge_mid[kk][None], near_edge[None]),
-                product(edge_far[kk][None], near_edge[None]),
+                product(edge_rows[:, :, cols], edge_rows[...]),
+                product(edge_mid[kk][None], near_edge) + level[0],
+                product(edge_far[kk][None], near_edge) + level[1],
             ]
             if mid:
-                extra.append(product(edge_end[:, kk], edge_rows[...]))
+                extra.append(product(edge_end[:, kk], edge_rows[...]) + level[2])
             for b in range(nb):
                 pt = acc[b, k] + extra[b]
                 p = jnp.transpose(pt).reshape(16, 2, 16, LANE)
@@ -533,13 +560,13 @@
                 o = 16 * (nb + b)
                 v = keep[k, o : o + 16] + take[k, o : o + 16].astype(F32)
                 mixed_t[k, :, 4 * b : 4 * b + 4] = v.astype(BF16).reshape(4, 4, 16, LANE)
-            red_d[kk, chip, 0:nb] = mixed_d[k, chip, 0:nb]
+            red_d[k, chip, 0:nb] = mixed_d[k, chip, 0:nb]
 
             def send_direct(step, carry):
                 to = (chip + step) % 16
                 copy_to(
                     mixed_d.at[k, to, 0:nb],
-                    red_d.at[kk, chip, 0:nb],
+                    red_d.at[k, chip, 0:nb],
                     dir_s.at[k],
                     dir_r.at[k],
                     (s, 2 * to + c, r),
@@ -561,38 +588,41 @@
 
             lax.fori_loop(1, 4, send_turned, 0)
 
-            @pl.when(k == 0)
-            def _():
+            if k == 0:
                 red_t[chip, 0 : 4 * nt] = mixed_t[k, x, 0 : 4 * nt]
-
-            @pl.when(k != 0)
-            def _():
+            else:
                 send_turned(0, 0)
 
-        def turn(k, carry):
-            emit(k)
-
-            @pl.when(k > 0)
-            def _():
-                spread(k - 1)
-
-            @pl.when(k == 1)
-            def _():
-                pass_mid(3)
-                pass_far(3)
-
-            @pl.when(k == 2)
-            def _():
-                products(3)
-
-            return carry
-
-        lax.fori_loop(0, 4, turn, 0)
+        def gather_step(k):
+            wait_bytes(red_d.at[0, 0:15, 0:nb], dir_r.at[k])
+            for yi in range(4):
+                part = red_d[k, 4 * yi, 0:nb].astype(F32)
+                for xi in range(1, 4):
+                    part = part + red_d[k, 4 * yi + xi, 0:nb].astype(F32)
+                j = (k + yi) % 4
+                if k == 0:
+                    tot[j, 0:nb] = part
+                else:
+                    tot[j, 0:nb] += part
+
+        emit(0)
+        pass_end(3)
+        pass_far(2)
+        send_end(7)
+        emit(1)
+        spread(0)
+        products(2)
+        pass_far(3)
+        emit(2)
+        spread(1)
+        products(3)
+        emit(3)
+        spread(2)
         lax.fori_loop(0, 22, put_column, 0)
         spread(3)
-
         for k in range(4):
-            wait_bytes(red_d.at[0, 0:15, 0:nb], dir_r.at[k])
+            gather_step(k)
+        for k in range(4):
             wait_bytes(red_t.at[0 : (3 if k == 0 else 4), 0 : 4 * nt], tra_r.at[k])
 
         for k in range(4):
@@ -600,10 +630,7 @@
             ln = slice(LANE * (k % 2), LANE * (k % 2) + LANE)
             rn = slice(8 * (k // 2), 8 * (k // 2) + 8)
 
-            def add_direct(i, acc):
-                return acc + red_d[k, i, 0:nb].astype(F32)
-
-            total = lax.fori_loop(1, 16, add_direct, red_d[k, 0, 0:nb].astype(F32))
+            total = tot[k, 0:nb]
             for q in range(2):
                 piece_d[q, :, ls] = total[0, 8 * q : 8 * q + 8]
                 for b in range(nt):
@@ -671,10 +698,13 @@
 
         for e in ends:
             e.wait_send()
+        if not mid:
+            wait_bytes(own.at[0, 0], str_s.at[0, chunk_of(3)])
+            wait_bytes(own.at[0, 0], str_s.at[1, chunk_of(3)])
         for k in range(4):
-            wait_bytes(own.at[0, 0], str_s.at[0, k])
-            wait_bytes(own.at[0, 0], str_s.at[1, k])
             if mid:
+                wait_bytes(own.at[0, 0], str_s.at[0, k])
+                wait_bytes(own.at[0, 0], str_s.at[1, k])
                 wait_bytes(own.at[0, 0], str_s.at[2, k])
                 wait_bytes(own.at[0, 0], str_s.at[3, k])
             wait_bytes(edge_own.at[0], edg_s.at[k]) if mid or k < 2 else None
@@ -735,6 +765,7 @@
             pltpu.VMEM((4, SIDE, LANE), F32),
             pltpu.VMEM((4, SIDE, LANE), F32),
             pltpu.VMEM((3, 22, SIDE, LANE), BF16),
+            pltpu.VMEM((3, 2, 64, LANE), F32),
             pltpu.VMEM((3, LANE, BLK), F32),
             pltpu.VMEM((4, 2, 11, SIDE, LANE), BF16),
             pltpu.VMEM((4, 2, 11, SIDE, LANE), BF16),
@@ -753,6 +784,7 @@
             pltpu.VMEM((4, 4, 12, 16, LANE), BF16),
             pltpu.VMEM((4, 16, 4, 16, LANE), BF16),
             pltpu.VMEM((16, 12, 16, LANE), BF16),
+            pltpu.VMEM((4, 4, 16, LANE), F32),
             pltpu.VMEM((2, 8, BLK), F32),
             pltpu.VMEM((2, 3, 16, 256), F32),
             pltpu.VMEM((2, 3, 16, 256), BF16),

time: 90.2 us -> 85.4 us (0.947)
  Pallas kernels: 84.1 us -> 79.2 us
    pallas_call x1, Pallas kernels: 84.1 us -> 79.2 us  [per_device(): pl.pallas_call(kernel, out_shape=(jax.ShapeDtypeStruct((1, ROWS, SIDE, BL...]
where the time goes in v3:
time: 85.4 us; the launch traced here: 85.2 us
  Pallas kernels  79.2 us (93%)
  local copies, waits for them, and re-layouts  4.76 us (6%)
    pallas_call x1, Pallas kernels, per_device(): pl.pallas_call(kernel, out_shape=(jax.ShapeDtypeStruct((1, ROWS, SIDE, BL...  79.2 us
    unnamed x6, local copies, waits for them, and re-layouts  4.55 us

profile of v3, /device:TPU:8, one launch (start us, length us, event | category | flops | bytes accessed | tf_op | source)
XLA Modules:
  0.0 85.2 jit_solution(9491920761582551616)
XLA Ops:
  0.6 0.8 copy.9
  1.4 0.1 reshape.10
  1.5 0.8 copy.10
  2.3 0.1 reshape.11
  2.4 0.6 pad_add_fusion.links
  3.0 79.2 %slope_gram.1 = (bf16[1,24,48,512]{3,2,1,0:T(8,128)(2,1)}, f32[8,2048]{1,0:T(8,128)}) custom-call(s32[128]{0:T(128)} %pad_add_fusion.links, bf16[1,24,48,512]{3,2,1,0:T(8,128)(2,1)} %field.1, s32[1,24,48]{2,1,0:T(8,128)} %mask.1, f32[1,24,48]{2,1,0:T(8,128)} %area.1), custom_call_target="tpu_custom_call" | custom-call | tf_op jit(solution)/shard_map/slope_gram/pallas_call | solution.py:742
  82.2 0.0 copy-start
  82.2 2.4 %copy.13 = bf16[1,24,48,512]{3,2,1,0:T(8,128)(2,1)} copy(bf16[1,24,48,512]{3,2,1,0:T(8,128)(2,1)} %get-tuple-element.4) | data formatting | bytes 2359296
  84.6 0.0 copy-done
  84.6 0.6 copy.14
Async XLA Ops:
  82.2 2.4 %copy-start = (f32[8,2048]{1,0:T(8,128)S(1)}, f32[8,2048]{1,0:T(8,128)}, u32[]{:S(2)}) copy-start(f32[8,2048]{1,0:T(8,128)} %get-tuple-element.5) | copy-start | bytes 196612

commit v4 on v3

--- a/solution.py
+++ b/solution.py
@@ -15,6 +15,7 @@
 SIDE = 48
 BLK = 512
 LANE = 128
+SHIFTS = (2, 1, 3, 0)
 GRAM_SCALE = 1.0 / (32 * 48 * 48)
 
 
@@ -73,6 +74,11 @@
     edge_mid,
     edge_far,
     acc,
+    keep_a,
+    give_a,
+    take_a,
+    mixed_a,
+    red_a,
     keep,
     give,
     take,
@@ -134,7 +140,8 @@
         pl.when(jnp.logical_not(is_mid))(do)
 
     def chunk_of(k):
-        return (k + y) % 4
+        turn = SHIFTS[k]
+        return (y + turn + (x % 2) * ((4 - 2 * turn) % 4)) % 4
 
     barrier = pltpu.get_barrier_semaphore()
 
@@ -219,14 +226,14 @@
             kk = chunk_of(k)
             copy_to(own.at[kk, hfar], mid_in.at[kk], str_s.at[0, kk], mid_r.at[kk], at_mid).start()
 
-    def send_end(n):
+    def send_end(k, far):
         @on_end
         def _():
-            if n >= 2:
-                wait_bytes(own.at[0, 0], str_s.at[n % 2, chunk_of(n // 2 - 1)])
-            kk = chunk_of(n // 2)
-            h = hnear if n % 2 else hfar
-            copy_to(own.at[kk, h], end_in.at[kk, h], str_s.at[n % 2, kk], end_r.at[kk, h], at_my_mid).start()
+            kk = chunk_of(k)
+            h = hfar if far else hnear
+            copy_to(
+                own.at[kk, h], end_in.at[kk, h], str_s.at[0 if far else 1, kk], end_r.at[kk, h], at_my_mid
+            ).start()
 
     def pass_end(k):
         @on_mid
@@ -250,8 +257,11 @@
             copy_to(far_in.at[kk], far_in.at[kk], str_s.at[3, kk], far_r.at[kk], at_end).start()
 
     send_sums(sums, 0)
-    send_mid(0)
-    send_end(0)
+    for k in range(4):
+        send_mid(k)
+        send_end(k, True)
+    send_end(0, False)
+    send_end(1, False)
 
     za.wait_recv()
     zb.wait_recv()
@@ -280,9 +290,7 @@
                 lines.at[p], gathered.at[p, c, a], halo_s.at[n], halo_r.at[n], (s, place(p, (a + step) % 4, b), r)
             ).start()
 
-    send_mid(1)
     pass_mid(0)
-    send_end(1)
 
     wait_sums(sums, 0)
     mean = (sums[0] + sums[1] + sums[2] + sums[3]) * (1.0 / SNAPS)
@@ -302,20 +310,17 @@
     lax.fori_loop(0, 22, inner_anomaly, 0)
     pass_end(0)
     pass_mid(1)
-    send_end(2)
 
     for p in range(2):
         a, b = here_on[p]
         for step in range(1, 4):
             wait_bytes(lines.at[p], halo_r.at[1 + 3 * p + step])
         copy_to(gathered.at[p, c], gathered.at[p, c], halo_s.at[8 + p], halo_r.at[8 + p], at_core).start()
-    send_mid(2)
-    pass_far(0)
-    send_end(3)
+    pass_mid(2)
 
     def request(tile, side_index):
-        u = links[2 * tile + side_index]
-        turn = links[64 + 2 * tile + side_index]
+        u = links[side_index, tile]
+        turn = links[2 + side_index, tile]
         return u // 8, (u // 2) % 4, u % 2, turn // 2, turn % 2
 
     for p in range(2):
@@ -337,9 +342,7 @@
             def _():
                 copy_to(chosen.at[p, bd, 1], arrived.at[p, b, 1], halo_s.at[n + 6], halo_r.at[n + 6], to).start()
 
-    pass_end(1)
-    pass_mid(2)
-    send_end(4)
+    pass_mid(3)
 
     def product(chunk, rows):
         k_size = chunk.shape[0] * chunk.shape[1]
@@ -367,16 +370,15 @@
     def _():
         level[2] = product(shift[2], anom[0, 0:22])
 
-    def products(k):
+    def early_product(k):
         kk = chunk_of(k)
         acc[0, k] = own_product(kk)
-
-        @on_end
-        def _():
-            wait_bytes(mid_in.at[kk], mid_r.at[kk])
-            wait_bytes(far_in.at[kk], far_r.at[kk])
-
+        on_end(lambda: wait_bytes(mid_in.at[kk], mid_r.at[kk]))
         acc[1, k] = inner_product(mid_in.at[kk], hnear)
+
+    def late_product(k):
+        kk = chunk_of(k)
+        on_end(lambda: wait_bytes(far_in.at[kk], far_r.at[kk]))
         acc[2, k] = inner_product(far_in.at[kk], hnear)
 
         @on_mid
@@ -384,7 +386,8 @@
             wait_bytes(end_in.at[kk, hnear], end_r.at[kk, hnear])
             acc[3, k] = inner_product(end_in.at[kk, 0], 0) + inner_product(end_in.at[kk, 1], 1)
 
-    products(0)
+    early_product(0)
+    early_product(1)
 
     for p in range(2):
         for step in range(1, 4):
@@ -452,15 +455,16 @@
     colsum = jnp.concatenate([esv, jnp.zeros((SIDE - ROWS, 1), F32)], axis=0)
     sums_e[s] = jnp.where(lane == 2, colsum, esum)
     send_sums(sums_e, 1)
-    send_mid(3)
-    pass_far(1)
-    send_end(5)
-    products(1)
+    send_end(2, False)
+    send_end(3, False)
+    pass_end(1)
+    pass_end(2)
+    early_product(2)
+    early_product(3)
+    pass_far(0)
 
     @on_mid
     def _():
-        wait_bytes(edge_end.at[0], edg_r.at[hfar])
-        copy_to(edge_end.at[hfar], edge_far, edg_s.at[1], edg_r.at[3], at_mid).start()
         wait_bytes(edge_mid, edg_r.at[2])
         copy_to(edge_mid, edge_mid, edg_s.at[2], edg_r.at[2], at_end).start()
 
@@ -476,9 +480,6 @@
         both = cells[h].astype(BF16)
         anom[0, i] = both[0:SIDE]
         edge_rows[h] = both
-    pass_end(2)
-    pass_mid(3)
-    send_end(6)
     shift_e[...] = jnp.zeros_like(shift_e)
     for h in range(2):
         w = column(weight_row(22 + h))
@@ -494,14 +495,8 @@
     @on_mid
     def _():
         level[2] += product(shift_e[2].astype(BF16), edge_rows[...])
-        wait_bytes(edge_far, edg_r.at[3])
-        copy_to(edge_far, edge_far, edg_s.at[3], edg_r.at[3], at_end).start()
-        wait_bytes(edge_end.at[0], edg_r.at[hnear])
-
-    @on_end
-    def _():
-        wait_bytes(edge_mid, edg_r.at[2])
-        wait_bytes(edge_far, edg_r.at[3])
+
+    on_end(lambda: wait_bytes(edge_mid, edg_r.at[2]))
 
     def put_column(i, carry):
         tile = anom[0, i, 32:48].astype(F32)
@@ -510,63 +505,92 @@
         return carry
 
     def plane(mid):
-        nb = 4 if mid else 3
-        nt = nb - 1
-
-        def emit(k):
+        nl = 2 if mid else 1
+        nt = 1 + nl
+
+        def block_of(b, k):
             kk = chunk_of(k)
             cols = pl.ds(pl.multiple_of(kk * LANE, LANE), LANE)
-            extra = [
-                product(edge_rows[:, :, cols], edge_rows[...]),
-                product(edge_mid[kk][None], near_edge) + level[0],
-                product(edge_far[kk][None], near_edge) + level[1],
-            ]
-            if mid:
-                extra.append(product(edge_end[:, kk], edge_rows[...]) + level[2])
-            for b in range(nb):
-                pt = acc[b, k] + extra[b]
-                p = jnp.transpose(pt).reshape(16, 2, 16, LANE)
-                for core in range(2):
-                    @pl.when(c == core)
-                    def _():
-                        keep[k, 16 * b : 16 * b + 16] = p[:, core]
-                        give[k, 16 * b : 16 * b + 16] = p[:, 1 - core].astype(BF16)
-                if b > 0:
-                    o = 16 * (nb + b - 1)
-                    pq = pt.reshape(4, 2, 16, BLK)
-                    for core in range(2):
-                        @pl.when(c == core)
-                        def _():
-                            for xd in range(4):
-                                for l in range(4):
-                                    ls = slice(LANE * l, LANE * l + LANE)
-                                    keep[k, o + 4 * xd + l] = pq[xd, core, :, ls]
-                                    give[k, o + 4 * xd + l] = pq[xd, 1 - core, :, ls].astype(BF16)
+            if b == 0:
+                extra = product(edge_rows[:, :, cols], edge_rows[...])
+            elif b == 1:
+                extra = product(edge_mid[kk][None], near_edge) + level[0]
+            elif b == 2:
+                extra = product(edge_far[kk][None], near_edge) + level[1]
+            else:
+                extra = product(edge_end[:, kk], edge_rows[...]) + level[2]
+            return acc[b, k] + extra
+
+        def put_straight(pt, keep_at, give_at, o):
+            p = jnp.transpose(pt).reshape(16, 2, 16, LANE)
+            for core in range(2):
+                @pl.when(c == core)
+                def _():
+                    keep_at[o : o + 16] = p[:, core]
+                    give_at[o : o + 16] = p[:, 1 - core].astype(BF16)
+
+        def put_turned(pt, keep_at, give_at, o):
+            pq = pt.reshape(4, 2, 16, BLK)
+            for core in range(2):
+                @pl.when(c == core)
+                def _():
+                    for xd in range(4):
+                        for l in range(4):
+                            ls = slice(LANE * l, LANE * l + LANE)
+                            keep_at[o + 4 * xd + l] = pq[xd, core, :, ls]
+                            give_at[o + 4 * xd + l] = pq[xd, 1 - core, :, ls].astype(BF16)
+
+        def emit_early():
+            for k in range(4):
+                put_straight(block_of(0, k), keep_a, give_a, 32 * k)
+                pt = block_of(1, k)
+                put_straight(pt, keep_a, give_a, 32 * k + 16)
+                put_turned(pt, keep_a, give_a, 128 + 16 * k)
+            copy_to(give_a, take_a, pair_s.at[4], pair_r.at[4], at_core).start()
+
+        def spread_early():
+            wait_bytes(take_a, pair_r.at[4])
+            for n in range(8):
+                o = 16 * n
+                mixed_a[:, n] = (keep_a[o : o + 16] + take_a[o : o + 16].astype(F32)).astype(BF16)
+            for k in range(4):
+                o = 128 + 16 * k
+                v = (keep_a[o : o + 16] + take_a[o : o + 16].astype(F32)).astype(BF16)
+                mixed_a[pl.ds(4 * chunk_of(k), 4), 8:12] = v.reshape(4, 4, 16, LANE)
+            red_a[chip] = mixed_a[chip]
+
+            def send(step, carry):
+                to = (chip + step) % 16
+                copy_to(mixed_a.at[to], red_a.at[chip], dir_s.at[4], dir_r.at[4], (s, 2 * to + c, r)).start()
+                return carry
+
+            lax.fori_loop(1, 16, send, 0)
+
+        def emit(k):
+            for i in range(nl):
+                pt = block_of(2 + i, k)
+                put_straight(pt, keep.at[k], give.at[k], 16 * i)
+                put_turned(pt, keep.at[k], give.at[k], 16 * (nl + i))
             copy_to(
-                give.at[k, 0 : 16 * (nb + nt)],
-                take.at[k, 0 : 16 * (nb + nt)],
-                pair_s.at[k],
-                pair_r.at[k],
-                at_core,
+                give.at[k, 0 : 32 * nl], take.at[k, 0 : 32 * nl], pair_s.at[k], pair_r.at[k], at_core
             ).start()
 
         def spread(k):
             kk = chunk_of(k)
-            wait_bytes(take.at[k, 0 : 16 * (nb + nt)], pair_r.at[k])
-            for b in range(nb):
+            wait_bytes(take.at[k, 0 : 32 * nl], pair_r.at[k])
+            for b in range(nl):
                 v = keep[k, 16 * b : 16 * b + 16] + take[k, 16 * b : 16 * b + 16].astype(F32)
                 mixed_d[k, :, b] = v.astype(BF16)
-            for b in range(nt):
-                o = 16 * (nb + b)
+                o = 16 * (nl + b)
                 v = keep[k, o : o + 16] + take[k, o : o + 16].astype(F32)
                 mixed_t[k, :, 4 * b : 4 * b + 4] = v.astype(BF16).reshape(4, 4, 16, LANE)
-            red_d[k, chip, 0:nb] = mixed_d[k, chip, 0:nb]
+            red_d[k, chip, 0:nl] = mixed_d[k, chip, 0:nl]
 
             def send_direct(step, carry):
                 to = (chip + step) % 16
                 copy_to(
-                    mixed_d.at[k, to, 0:nb],
-                    red_d.at[k, chip, 0:nb],
+                    mixed_d.at[k, to, 0:nl],
+                    red_d.at[k, chip, 0:nl],
                     dir_s.at[k],
                     dir_r.at[k],
                     (s, 2 * to + c, r),
@@ -578,8 +602,8 @@
             def send_turned(step, carry):
                 xd = (x + step) % 4
                 copy_to(
-                    mixed_t.at[k, xd, 0 : 4 * nt],
-                    red_t.at[chip, 0 : 4 * nt],
+                    mixed_t.at[k, xd, 0 : 4 * nl],
+                    red_t.at[chip, 0 : 4 * nl],
                     tra_s.at[k],
                     tra_r.at[k],
                     (s, face_of(kk, xd, c), r),
@@ -587,59 +611,90 @@
                 return carry
 
             lax.fori_loop(1, 4, send_turned, 0)
-
-            if k == 0:
-                red_t[chip, 0 : 4 * nt] = mixed_t[k, x, 0 : 4 * nt]
+            if SHIFTS[k] == 0:
+                red_t[chip, 0 : 4 * nl] = mixed_t[k, x, 0 : 4 * nl]
             else:
                 send_turned(0, 0)
 
+        def column_of(k, yi, odd):
+            return (yi + (4 - SHIFTS[k] if odd else SHIFTS[k])) % 4
+
+        def gather_early():
+            wait_bytes(red_a.at[0:15], dir_r.at[4])
+            for k in range(4):
+                for yi in range(4):
+                    for odd in range(2):
+                        rows = slice(2 * k, 2 * k + 2)
+                        part = red_a[4 * yi + odd, rows].astype(F32) + red_a[4 * yi + 2 + odd, rows].astype(F32)
+                        j = column_of(k, yi, odd)
+                        if k == 0 and odd == 0:
+                            tot[j, 0:2] = part
+                        else:
+                            tot[j, 0:2] += part
+
         def gather_step(k):
-            wait_bytes(red_d.at[0, 0:15, 0:nb], dir_r.at[k])
+            wait_bytes(red_d.at[0, 0:15, 0:nl], dir_r.at[k])
             for yi in range(4):
-                part = red_d[k, 4 * yi, 0:nb].astype(F32)
-                for xi in range(1, 4):
-                    part = part + red_d[k, 4 * yi + xi, 0:nb].astype(F32)
-                j = (k + yi) % 4
-                if k == 0:
-                    tot[j, 0:nb] = part
-                else:
-                    tot[j, 0:nb] += part
-
+                for odd in range(2):
+                    part = red_d[k, 4 * yi + odd, 0:nl].astype(F32) + red_d[k, 4 * yi + 2 + odd, 0:nl].astype(F32)
+                    j = column_of(k, yi, odd)
+                    if k == 0 and odd == 0:
+                        tot[j, 2 : 2 + nl] = part
+                    else:
+                        tot[j, 2 : 2 + nl] += part
+
+        emit_early()
+        if mid:
+            wait_bytes(edge_end.at[0], edg_r.at[hfar])
+            copy_to(edge_end.at[hfar], edge_far, edg_s.at[1], edg_r.at[3], at_mid).start()
+        pass_end(3)
+        pass_far(1)
+        spread_early()
+        late_product(0)
+        late_product(1)
+        pass_far(2)
+        wait_bytes(edge_far, edg_r.at[3])
+        if mid:
+            copy_to(edge_far, edge_far, edg_s.at[3], edg_r.at[3], at_end).start()
+            wait_bytes(edge_end.at[0], edg_r.at[hnear])
         emit(0)
-        pass_end(3)
-        pass_far(2)
-        send_end(7)
         emit(1)
         spread(0)
-        products(2)
         pass_far(3)
+        spread(1)
+        late_product(2)
         emit(2)
-        spread(1)
-        products(3)
+        late_product(3)
         emit(3)
         spread(2)
         lax.fori_loop(0, 22, put_column, 0)
         spread(3)
+        gather_early()
         for k in range(4):
             gather_step(k)
         for k in range(4):
-            wait_bytes(red_t.at[0 : (3 if k == 0 else 4), 0 : 4 * nt], tra_r.at[k])
+            wait_bytes(red_t.at[0 : (4 if SHIFTS[k] else 3), 0 : 4 * nl], tra_r.at[k])
 
         for k in range(4):
             ls = slice(LANE * k, LANE * k + LANE)
             ln = slice(LANE * (k % 2), LANE * (k % 2) + LANE)
             rn = slice(8 * (k // 2), 8 * (k // 2) + 8)
 
-            total = tot[k, 0:nb]
+            total = tot[k, 0 : 1 + nt]
             for q in range(2):
                 piece_d[q, :, ls] = total[0, 8 * q : 8 * q + 8]
                 for b in range(nt):
                     piece_n[q, b, rn, ln] = total[1 + b, 8 * q : 8 * q + 8]
 
+        def add_early(i, acc):
+            return acc + red_a[i, 8:12].astype(F32)
+
         def add_turned(i, acc):
-            return acc + red_t[i, 0 : 4 * nt].astype(F32)
-
-        total = lax.fori_loop(1, 16, add_turned, red_t[0, 0 : 4 * nt].astype(F32))
+            return acc + red_t[i, 0 : 4 * nl].astype(F32)
+
+        first_sum = lax.fori_loop(1, 16, add_early, red_a[0, 8:12].astype(F32))
+        rest_sum = lax.fori_loop(1, 16, add_turned, red_t[0, 0 : 4 * nl].astype(F32))
+        total = jnp.concatenate([first_sum, rest_sum], axis=0)
         for b in range(nt):
             for q in range(2):
                 rows = slice(8 * q, 8 * q + 8)
@@ -698,19 +753,18 @@
 
         for e in ends:
             e.wait_send()
-        if not mid:
-            wait_bytes(own.at[0, 0], str_s.at[0, chunk_of(3)])
-            wait_bytes(own.at[0, 0], str_s.at[1, chunk_of(3)])
         for k in range(4):
+            wait_bytes(own.at[0, 0], str_s.at[0, k])
+            wait_bytes(own.at[0, 0], str_s.at[1, k])
             if mid:
-                wait_bytes(own.at[0, 0], str_s.at[0, k])
-                wait_bytes(own.at[0, 0], str_s.at[1, k])
                 wait_bytes(own.at[0, 0], str_s.at[2, k])
                 wait_bytes(own.at[0, 0], str_s.at[3, k])
             wait_bytes(edge_own.at[0], edg_s.at[k]) if mid or k < 2 else None
-            wait_bytes(give.at[k, 0 : 16 * (nb + nt)], pair_s.at[k])
-            wait_bytes(mixed_d.at[0, 0:15, 0:nb], dir_s.at[k])
-            wait_bytes(red_t.at[0 : (3 if k == 0 else 4), 0 : 4 * nt], tra_s.at[k])
+            wait_bytes(give.at[k, 0 : 32 * nl], pair_s.at[k])
+            wait_bytes(mixed_d.at[0, 0:15, 0:nl], dir_s.at[k])
+            wait_bytes(red_t.at[0 : (4 if SHIFTS[k] else 3), 0 : 4 * nl], tra_s.at[k])
+        wait_bytes(give_a, pair_s.at[4])
+        wait_bytes(mixed_a.at[0:15], dir_s.at[4])
 
     @on_mid
     def _():
@@ -738,7 +792,7 @@
     vmem = pl.BlockSpec(memory_space=pltpu.VMEM)
     smem = pl.BlockSpec(memory_space=pltpu.SMEM)
     dma = pltpu.SemaphoreType.DMA
-    links = jnp.concatenate([tile_links.reshape(-1), edge_turns.reshape(-1)])
+    links = jnp.concatenate([tile_links.T, edge_turns.T], axis=0)
     return pl.pallas_call(
         kernel,
         out_shape=(
@@ -777,13 +831,18 @@
             pltpu.VMEM((4, 64, LANE), BF16),
             pltpu.VMEM((4, 64, LANE), BF16),
             pltpu.VMEM((4, 4, LANE, BLK), F32),
-            pltpu.VMEM((4, 112, 16, LANE), F32),
-            pltpu.VMEM((4, 112, 16, LANE), BF16),
-            pltpu.VMEM((4, 112, 16, LANE), BF16),
-            pltpu.VMEM((4, 16, 4, 16, LANE), BF16),
-            pltpu.VMEM((4, 4, 12, 16, LANE), BF16),
-            pltpu.VMEM((4, 16, 4, 16, LANE), BF16),
+            pltpu.VMEM((192, 16, LANE), F32),
+            pltpu.VMEM((192, 16, LANE), BF16),
+            pltpu.VMEM((192, 16, LANE), BF16),
             pltpu.VMEM((16, 12, 16, LANE), BF16),
+            pltpu.VMEM((16, 12, 16, LANE), BF16),
+            pltpu.VMEM((4, 64, 16, LANE), F32),
+            pltpu.VMEM((4, 64, 16, LANE), BF16),
+            pltpu.VMEM((4, 64, 16, LANE), BF16),
+            pltpu.VMEM((4, 16, 2, 16, LANE), BF16),
+            pltpu.VMEM((4, 4, 8, 16, LANE), BF16),
+            pltpu.VMEM((4, 16, 2, 16, LANE), BF16),
+            pltpu.VMEM((16, 8, 16, LANE), BF16),
             pltpu.VMEM((4, 4, 16, LANE), F32),
             pltpu.VMEM((2, 8, BLK), F32),
             pltpu.VMEM((2, 3, 16, 256), F32),
@@ -802,10 +861,10 @@
             dma((4,)),
             dma((4,)),
             dma((4,)),
-            dma((4,)),
-            dma((4,)),
-            dma((4,)),
-            dma((4,)),
+            dma((5,)),
+            dma((5,)),
+            dma((5,)),
+            dma((5,)),
             dma((4,)),
             dma((4,)),
             dma((8,)),

time: 85.4 us -> 82.3 us (0.964); the launches traced: 85.2 us -> 80.7 us
  Pallas kernels: 79.2 us -> 75.7 us
  local copies, waits for them, and re-layouts: 4.76 us -> 3.03 us
    pallas_call x1, Pallas kernels: 79.2 us -> 75.7 us  [per_device(): pl.pallas_call(kernel, out_shape=(jax.ShapeDtypeStruct((1, ROWS, SIDE, BL...]
    unnamed x6 -> x4, local copies, waits for them, and re-layouts: 4.55 us -> 3.03 us
where the time goes in v4:
time: 82.3 us; the launch traced here: 80.7 us
  Pallas kernels  75.7 us (92%)
  local copies, waits for them, and re-layouts  3.03 us (4%)
  other arithmetic  1.28 us (2%)
    pallas_call x1, Pallas kernels, per_device(): pl.pallas_call(kernel, out_shape=(jax.ShapeDtypeStruct((1, ROWS, SIDE, BL...  75.7 us
    unnamed x4, local copies, waits for them, and re-layouts  3.03 us

profile of v4, /device:TPU:8, one launch (start us, length us, event | category | flops | bytes accessed | tf_op | source)
XLA Modules:
  0.0 80.7 jit_solution(3186866876855563066)
XLA Ops:
  0.6 1.3 %pad_add_fusion.links = s32[4,32]{1,0:T(4,128)} fusion(s32[2,32]{1,0:T(2,128)} %bitcast.2, s32[2,32]{1,0:T(2,128)} %bitcast.3), kind=kLoop, calls=%fused_computation | loop fusion | flops 128 | bytes 1024 | tf_op jit(solution)/shard_map/concatenate | solution.py:795
  1.9 75.7 %slope_gram.1 = (bf16[1,24,48,512]{3,2,1,0:T(8,128)(2,1)}, f32[8,2048]{1,0:T(8,128)}) custom-call(s32[4,32]{1,0:T(4,128)} %pad_add_fusion.links, bf16[1,24,48,512]{3,2,1,0:T(8,128)(2,1)} %field.1, s32[1,24,48]{2,1,0:T(8,128)} %mask.1, f32[1,24,48]{2,1,0:T(8,128)} %area.1), custom_call_target="tpu_custom_call" | custom-call | tf_op jit(solution)/shard_map/slope_gram/pallas_call | solution.py:796
  77.6 0.0 copy-start
  77.6 2.4 %copy.9 = bf16[1,24,48,512]{3,2,1,0:T(8,128)(2,1)} copy(bf16[1,24,48,512]{3,2,1,0:T(8,128)(2,1)} %get-tuple-element.4) | data formatting | bytes 2359296
  80.0 0.0 copy-done
  80.0 0.6 copy.10
Async XLA Ops:
  77.6 2.4 %copy-start = (f32[8,2048]{1,0:T(8,128)S(1)}, f32[8,2048]{1,0:T(8,128)}, u32[]{:S(2)}) copy-start(f32[8,2048]{1,0:T(8,128)} %get-tuple-element.5) | copy-start | bytes 196612

commit v5 on v4

--- a/solution.py
+++ b/solution.py
@@ -643,6 +643,48 @@
                     else:
                         tot[j, 2 : 2 + nl] += part
 
+        def fold(b):
+            for k in range(4):
+                ls = slice(LANE * k, LANE * k + LANE)
+                ln = slice(LANE * (k % 2), LANE * (k % 2) + LANE)
+                rn = slice(8 * (k // 2), 8 * (k // 2) + 8)
+                for q in range(2):
+                    if b == 0:
+                        piece_d[q, :, ls] = tot[k, 0, 8 * q : 8 * q + 8]
+                    piece_n[q, b, rn, ln] = tot[k, 1 + b, 8 * q : 8 * q + 8]
+            mixed_n[b] = piece_n[1 - r, b].astype(BF16)
+
+        def fold_turned(b, total):
+            for q in range(2):
+                parts = [total[l, 8 * q : 8 * q + 8] for l in range(4)]
+                top = jnp.concatenate(parts[0:2], axis=1)
+                bottom = jnp.concatenate(parts[2:4], axis=1)
+                piece_t[q, b] = jnp.concatenate([top, bottom], axis=0).astype(BF16)
+
+        def add_early(i, acc):
+            return acc + red_a[i, 8:12].astype(F32)
+
+        def add_turned(i, acc):
+            return acc + red_t[i, 0 : 4 * nl].astype(F32)
+
+        def send_last(b):
+            copies = [copy_to(mixed_n.at[b], fin_n.at[b], fin_s.at[7 + b], fin_r.at[9 + b], other_row)]
+            if b == 0:
+                copies.append(copy_to(piece_d.at[1 - r], fin_d, fin_s.at[0], fin_r.at[0], other_row))
+            for q in range(2):
+                copies.append(
+                    copy_to(
+                        piece_t.at[q, b],
+                        fin_t.at[s, r],
+                        fin_s.at[1 + 2 * b + q],
+                        fin_r.at[1 + 2 * s + r],
+                        (others_of[b], f, q),
+                    )
+                )
+            for e in copies:
+                e.start()
+                ends.append(e)
+
         emit_early()
         if mid:
             wait_bytes(edge_end.at[0], edg_r.at[hfar])
@@ -667,65 +709,28 @@
         late_product(3)
         emit(3)
         spread(2)
-        lax.fori_loop(0, 22, put_column, 0)
         spread(3)
         gather_early()
+        ends = []
+        others_of = [other_mid, other_end] + ([my_end] if mid else [])
+        fold(0)
+        fold_turned(0, lax.fori_loop(1, 16, add_early, red_a[0, 8:12].astype(F32)))
+        send_last(0)
+        lax.fori_loop(0, 22, put_column, 0)
         for k in range(4):
             gather_step(k)
         for k in range(4):
             wait_bytes(red_t.at[0 : (4 if SHIFTS[k] else 3), 0 : 4 * nl], tra_r.at[k])
 
-        for k in range(4):
-            ls = slice(LANE * k, LANE * k + LANE)
-            ln = slice(LANE * (k % 2), LANE * (k % 2) + LANE)
-            rn = slice(8 * (k // 2), 8 * (k // 2) + 8)
-
-            total = tot[k, 0 : 1 + nt]
-            for q in range(2):
-                piece_d[q, :, ls] = total[0, 8 * q : 8 * q + 8]
-                for b in range(nt):
-                    piece_n[q, b, rn, ln] = total[1 + b, 8 * q : 8 * q + 8]
-
-        def add_early(i, acc):
-            return acc + red_a[i, 8:12].astype(F32)
-
-        def add_turned(i, acc):
-            return acc + red_t[i, 0 : 4 * nl].astype(F32)
-
-        first_sum = lax.fori_loop(1, 16, add_early, red_a[0, 8:12].astype(F32))
+        for b in range(1, nt):
+            fold(b)
         rest_sum = lax.fori_loop(1, 16, add_turned, red_t[0, 0 : 4 * nl].astype(F32))
-        total = jnp.concatenate([first_sum, rest_sum], axis=0)
+        for b in range(1, nt):
+            fold_turned(b, rest_sum[4 * b - 4 : 4 * b])
+            send_last(b)
+        wait_bytes(fin_d, fin_r.at[0])
         for b in range(nt):
-            for q in range(2):
-                rows = slice(8 * q, 8 * q + 8)
-                parts = [total[4 * b + l, rows] for l in range(4)]
-                top = jnp.concatenate(parts[0:2], axis=1)
-                bottom = jnp.concatenate(parts[2:4], axis=1)
-                piece_t[q, b] = jnp.concatenate([top, bottom], axis=0).astype(BF16)
-        for b in range(nt):
-            mixed_n[b] = piece_n[1 - r, b].astype(BF16)
-
-        ends = []
-        e = copy_to(piece_d.at[1 - r], fin_d, fin_s.at[0], fin_r.at[0], other_row)
-        e.start()
-        ends.append(e)
-        e = copy_to(mixed_n.at[0:nt], fin_n.at[0:nt], fin_s.at[7], fin_r.at[9], other_row)
-        e.start()
-        ends.append(e)
-        others_of = [other_mid, other_end] + ([my_end] if mid else [])
-        for b in range(nt):
-            for q in range(2):
-                e = copy_to(
-                    piece_t.at[q, b],
-                    fin_t.at[s, r],
-                    fin_s.at[1 + 2 * b + q],
-                    fin_r.at[1 + 2 * s + r],
-                    (others_of[b], f, q),
-                )
-                e.start()
-                ends.append(e)
-        wait_bytes(fin_d, fin_r.at[0])
-        wait_bytes(fin_n.at[0:nt], fin_r.at[9])
+            wait_bytes(fin_n.at[b], fin_r.at[9 + b])
         sources = [other_mid, other_end] + ([] if mid else [my_mid])
         for p in sources:
             for q in range(2):
@@ -867,8 +872,8 @@
             dma((5,)),
             dma((4,)),
             dma((4,)),
-            dma((8,)),
             dma((10,)),
+            dma((12,)),
         ],
         compiler_params=pltpu.CompilerParams(
             collective_id=0, has_side_effects=True, vmem_limit_bytes=56 * 1024 * 1024

time: 82.3 us -> 81.4 us (0.989)
  no operation moved by 1% of the time
where the time goes in v5:
time: 81.4 us; the launch traced here: 80.1 us
  Pallas kernels  75.2 us (92%)
  local copies, waits for them, and re-layouts  3.03 us (4%)
  other arithmetic  1.28 us (2%)
    pallas_call x1, Pallas kernels, per_device(): pl.pallas_call(kernel, out_shape=(jax.ShapeDtypeStruct((1, ROWS, SIDE, BL...  75.2 us
    unnamed x4, local copies, waits for them, and re-layouts  3.03 us

profile of v5, /device:TPU:8, one launch (start us, length us, event | category | flops | bytes accessed | tf_op | source)
XLA Modules:
  0.0 80.1 jit_solution(2210522919295054272)
XLA Ops:
  0.6 1.3 %pad_add_fusion.links = s32[4,32]{1,0:T(4,128)} fusion(s32[2,32]{1,0:T(2,128)} %bitcast.2, s32[2,32]{1,0:T(2,128)} %bitcast.3), kind=kLoop, calls=%fused_computation | loop fusion | flops 128 | bytes 1024 | tf_op jit(solution)/shard_map/concatenate | solution.py:800
  1.9 75.2 %slope_gram.1 = (bf16[1,24,48,512]{3,2,1,0:T(8,128)(2,1)}, f32[8,2048]{1,0:T(8,128)}) custom-call(s32[4,32]{1,0:T(4,128)} %pad_add_fusion.links, bf16[1,24,48,512]{3,2,1,0:T(8,128)(2,1)} %field.1, s32[1,24,48]{2,1,0:T(8,128)} %mask.1, f32[1,24,48]{2,1,0:T(8,128)} %area.1), custom_call_target="tpu_custom_call" | custom-call | tf_op jit(solution)/shard_map/slope_gram/pallas_call | solution.py:801
  77.1 0.0 copy-start
  77.1 2.4 %copy.9 = bf16[1,24,48,512]{3,2,1,0:T(8,128)(2,1)} copy(bf16[1,24,48,512]{3,2,1,0:T(8,128)(2,1)} %get-tuple-element.4) | data formatting | bytes 2359296
  79.5 0.0 copy-done
  79.5 0.6 copy.10
Async XLA Ops:
  77.1 2.4 %copy-start = (f32[8,2048]{1,0:T(8,128)S(1)}, f32[8,2048]{1,0:T(8,128)}, u32[]{:S(2)}) copy-start(f32[8,2048]{1,0:T(8,128)} %get-tuple-element.5) | copy-start | bytes 196612
